TPU v7x, 256 devices: a whole 4x4x8 slice. The times are simulated.
256 devices in a mesh: grp: 8 (over z_hi, core), seq: 32 (over z_lo, y, x).
Axes of the slice: x: 4, y: 4, z: 8 (z_hi: 4, z_lo: 2; z = z_hi * 2 + z_lo), core: 2. Of those that a mesh axis runs over, the one named last changes fastest.
Arguments:
- query: bfloat16 [65536, 512], P(('grp', 'seq')), may hold values from -16 to 16
- key_in: bfloat16 [65536, 512], P(('grp', 'seq')), may hold values from -16 to 16
- value_in: bfloat16 [65536, 512], P(('grp', 'seq')), may hold values from -16 to 16
- grad_out: bfloat16 [65536, 512], P(('grp', 'seq')), may hold values from -6 to 6
Outputs:
- output: bfloat16 [65536, 512], P(('grp', 'seq'))
- grad_query: bfloat16 [65536, 512], P(('grp', 'seq'))
- grad_key: bfloat16 [65536, 512], P(('grp', 'seq'))
- grad_value: bfloat16 [65536, 512], P(('grp', 'seq'))
All inputs are finite; a program needn't handle non-finite values.
Results may differ from a plain program's by a relative error of at most 0.018.
Values may be sent and summed in bfloat16 or wider, within the bound.
A program may use at most 128 MiB of HBM per device.

v0:
```python
import functools

import jax
import jax.numpy as jnp
from jax import lax
from jax.experimental import pallas as pl
from jax.experimental.pallas import tpu as pltpu
from jax.sharding import PartitionSpec as P

MESH = pl.DeviceIdType.MESH
F32 = jnp.float32
BF16 = jnp.bfloat16
LANES = 128
NT = (((1,), (1,)), ((), ()))
TN = (((0,), (0,)), ((), ()))


def flip(value, mask, bits):
    out = 0
    for bit in range(bits):
        own = (value // 2**bit) % 2
        if isinstance(mask, int):
            out = out + 2**bit * (1 - own if (mask >> bit) & 1 else own)
        else:
            out = out + 2**bit * ((own + (mask // 2**bit) % 2) % 2)
    return out


def iota(shape, dim):
    return lax.broadcasted_iota(jnp.int32, shape, dim)


def shr(value, amount):
    return jnp.right_shift(value, amount)


def mm(a, b):
    return jnp.dot(a, b, preferred_element_type=F32)


def mm_nt(a, b):
    return lax.dot_general(a, b, NT, preferred_element_type=F32)


def mm_tn(a, b):
    return lax.dot_general(a, b, TN, preferred_element_type=F32)


def pool_matrix(rows, weight=0.5):
    shape = (rows // 2, rows)
    return jnp.where(shr(iota(shape, 1), 1) == iota(shape, 0), weight, 0.0).astype(BF16)


def spread_matrix(rows, weight):
    shape = (2 * rows, rows)
    return jnp.where(shr(iota(shape, 0), 1) == iota(shape, 1), weight, 0.0).astype(BF16)


def coarsen(values):
    return mm(pool_matrix(values.shape[0]), values).astype(BF16)


def lane_low():
    return iota((1, LANES), 1) < 64


def head_masks(weight):
    low = lane_low()
    return (
        jnp.where(low, weight, 0.0).astype(BF16),
        jnp.where(low, 0.0, weight).astype(BF16),
    )


def with_ones(vals):
    return jnp.concatenate([vals, jnp.ones_like(vals)], axis=1)


def fold(stacked, rows):
    return jnp.where(lane_low(), stacked[:rows], stacked[rows:])


def split2(values):
    high = values.astype(BF16)
    return high, (values - high.astype(F32)).astype(BF16)


def stack_heads(q):
    low, high = head_masks(0.125)
    return jnp.concatenate([q * low, q * high], axis=0)


def soft_weights(scores):
    peak = jnp.max(scores, axis=1, keepdims=True).astype(BF16).astype(F32)
    return jnp.exp(scores - peak).astype(BF16), peak


def attend(q, kv):
    rows = q.shape[0]
    scores = mm_nt(stack_heads(q), kv[:, :LANES])
    weights, peak = soft_weights(scores)
    both = mm(weights, with_ones(kv[:, LANES:]))
    weighted = fold(both[:, :LANES], rows)
    total = fold(both[:, LANES:], rows)
    wide = jnp.broadcast_to(peak, (2 * rows, LANES))
    return weights, fold(wide, rows), weighted, total


def stack_grads(gw, gt):
    low, high = head_masks(1.0)
    lane = iota((1, LANES), 1)
    first = jnp.where((lane == 0) | (lane == 64), 1.0, 0.0).astype(BF16)
    second = jnp.where((lane == 1) | (lane == 65), 1.0, 0.0).astype(BF16)
    gt_high, gt_low = split2(gt)
    extra = gt_high * first + gt_low * second
    return jnp.concatenate(
        [
            jnp.concatenate([gw * low, extra * low], axis=1),
            jnp.concatenate([gw * high, extra * high], axis=1),
        ],
        axis=0,
    )


def attend_back(q, kv, weights, gw, gt):
    rows = q.shape[0]
    stacked = stack_grads(gw, gt)
    lift = mm_nt(stacked, with_ones(kv[:, LANES:]))
    gs = (weights.astype(F32) * lift).astype(BF16)
    gv = mm_tn(weights, stacked[:, :LANES])
    gk = mm_tn(gs, stack_heads(q))
    gq = fold(mm(gs, kv[:, :LANES]), rows) * 0.125
    return gq, jnp.concatenate([gk, gv], axis=1)


OFFS = (0, 64, 96, 112, 120)


def row_level(row):
    level = jnp.zeros_like(row)
    for edge in OFFS[1:]:
        level = level + jnp.where(row >= edge, 1, 0)
    return level


def pick(full, level, width=LANES):
    out = jnp.where(level == 0, full[:, :width], 0.0)
    for index in range(1, 5):
        out = jnp.where(level == index, full[:, index * width : (index + 1) * width], out)
    return out


def blocks_of(values, level):
    zero = jnp.zeros_like(values)
    return jnp.concatenate([jnp.where(level == i, values, zero) for i in range(5)], axis=1)


def level_spread():
    parts = []
    shape = (LANES, LANES)
    row, col = iota(shape, 0), iota(shape, 1)
    for index, start in enumerate(OFFS):
        parts.append(jnp.where(col == start + shr(row, index + 1), 1.0, 0.0))
    return parts


def level_pool():
    parts = []
    shape = (LANES, LANES)
    row, col = iota(shape, 0), iota(shape, 1)
    for index, start in enumerate(OFFS):
        parts.append(jnp.where(row == start + shr(col, index + 1), 1.0, 0.0))
    return jnp.concatenate(parts, axis=1).astype(BF16)


def kernel(
    q_ref, k_ref, v_ref, g_ref, out_ref, gq_ref, gk_ref, gv_ref,
    qb, kvb, gb, l3, l4, kv3own, kv3sib, r4, own5, own6, own7, own8, rf,
    qp, kvp, w0, w1, w0w, w0p, w0t, w1w, w1p, w1t,
    a1, b1, m1, n1, d1, gw0, gt0, gw1, gt1, spm, spn, spd, g1s, d1s, g2s, d2s,
    ob, oq, bk, bkr, gq1, gkv1, gkv2, sb, rb, t4, m3s, m4s, cb, g4s,
    p_send, p_recv, a_send, a_recv, b_send, b_recv, bb_send, bb_recv, aa_send, aa_recv,
    o_send, o_recv, loc,
):
    grp, seq = lax.axis_index("grp"), lax.axis_index("seq")
    x, y = seq % 4, (seq // 4) % 4
    w = grp * 2 + seq // 16
    y_pair, y_bit = y // 2, y % 2
    sib = flip(y, 1, 2)

    def place(px, py, pw):
        return (pw // 2, (pw % 2) * 16 + py * 4 + px)

    def remote(src, dst, send, recv, device):
        return pltpu.make_async_remote_copy(
            src_ref=src, dst_ref=dst, send_sem=send, recv_sem=recv,
            device_id=device, device_id_type=MESH,
        )

    plane = [(mx, my) for my in (1, 2, 3, 0) for mx in range(4) if (mx, my) != (0, 0)]

    barrier = pltpu.get_barrier_semaphore()
    for mx, my in plane:
        pl.semaphore_signal(
            barrier, inc=1, device_id=place(flip(x, mx, 2), flip(y, my, 2), w), device_id_type=MESH
        )
    for m in range(1, 16):
        pl.semaphore_signal(
            barrier, inc=1, device_id=place(x, y, flip(w, m, 4)), device_id_type=MESH
        )

    for part, ref in ((0, k_ref), (1, v_ref)):
        rows = coarsen(coarsen(coarsen(ref[...])))
        upper = coarsen(rows)
        for j in range(4):
            l3[j, :, part * LANES : (part + 1) * LANES] = rows[:, j * LANES : (j + 1) * LANES]
            l4[j, :, part * LANES : (part + 1) * LANES] = upper[:, j * LANES : (j + 1) * LANES]

    pl.semaphore_wait(barrier, 30)

    stage_a = []
    for index, (mx, my) in enumerate(plane):
        px, py = flip(x, mx, 2), flip(y, my, 2)
        if my == 0:
            src, dst = l3.at[px], kv3own.at[x]
        elif my == 1:
            src, dst = l3.at[px], kv3sib.at[x]
        else:
            src, dst = l4.at[px], r4.at[y, x]
        copy = remote(src, dst, a_send.at[index], a_recv.at[index], place(px, py, w))
        copy.start()
        stage_a.append(copy)

    def lanes(index):
        return pl.ds(pl.multiple_of(index * LANES, LANES), LANES)

    def token_copies(mask):
        px = flip(x, mask, 2)
        device = place(px, y, w)
        pairs = (
            (k_ref, kvb.at[x, :, pl.ds(0, LANES)]),
            (v_ref, kvb.at[x, :, pl.ds(LANES, LANES)]),
            (q_ref, qb.at[x]),
            (g_ref, gb.at[x]),
        )
        return [
            remote(
                ref.at[:, lanes(px)], dst, p_send.at[i, mask - 1], p_recv.at[i, mask - 1], device
            )
            for i, (ref, dst) in enumerate(pairs)
        ]

    moves = [token_copies(mask) for mask in (1, 2, 3)]
    for i in range(4):
        for copies in moves:
            copies[i].start()

    kvb[x, :, :LANES] = k_ref[:, lanes(x)]
    kvb[x, :, LANES:] = v_ref[:, lanes(x)]
    qb[x] = q_ref[:, lanes(x)]
    gb[x] = g_ref[:, lanes(x)]
    kv3own[x] = l3[x]

    def chunk_forward(slot):
        q, kv = qb[slot], kvb[slot]
        weights, peak, weighted, total = attend(q, kv)
        w0[slot] = weights
        w0p[slot], w0w[slot], w0t[slot] = peak, weighted, total
        qp[slot] = coarsen(q)
        kvp[slot] = coarsen(kv)

    chunk_forward(x)

    for copy in stage_a:
        copy.wait_recv()
    half = pool_matrix(LANES)
    r4[y] = mm(half, kv3own[...].reshape(LANES, 256)).astype(BF16).reshape(4, 16, 256)
    r4[sib] = mm(half, kv3sib[...].reshape(LANES, 256)).astype(BF16).reshape(4, 16, 256)
    kvp[7] = kv3sib[...].reshape(LANES, 256)
    rows5 = coarsen(r4[...].reshape(256, 256))
    rows6 = coarsen(rows5)
    rows7 = coarsen(rows6)
    rows8 = coarsen(rows7)
    own5[...] = rows5.reshape(8, 16, 256)
    own6[...] = rows6.reshape(4, 16, 256)
    own7[...] = rows7.reshape(2, 16, 256)
    own8[...] = rows8.reshape(1, 16, 256)

    stage_b = []
    owns = (own5, own6, own7, own8)
    for m in range(1, 16):
        up = m.bit_length() - 1
        count = 8 >> up
        start = 8 * up + (w % 2**up) * count
        copy = remote(
            owns[up], rf.at[pl.ds(start, count)], b_send.at[m - 1], b_recv.at[m - 1],
            place(x, y, flip(w, m, 4)),
        )
        copy.start()
        stage_b.append(copy)

    def chunk_step(mask, carry):
        px = flip(x, mask, 2)
        for copy in token_copies(mask)[:3]:
            copy.wait_recv()
        chunk_forward(px)
        return carry

    lax.fori_loop(1, 4, chunk_step, 0)

    qp[4] = coarsen(qp[0:2].reshape(256, LANES))
    qp[5] = coarsen(qp[2:4].reshape(256, LANES))
    kvp[4] = coarsen(kvp[0:2].reshape(256, 256))
    kvp[5] = coarsen(kvp[2:4].reshape(256, 256))
    qp[6] = coarsen(qp[4:6].reshape(256, LANES))

    def unit_step(unit, carry):
        other = unit + 1 - 2 * (unit % 2)
        weights, peak, weighted, total = attend(qp[unit], kvp[other])
        w1[unit] = weights
        w1p[unit], w1w[unit], w1t[unit] = peak, weighted, total
        return carry

    lax.fori_loop(0, 7, unit_step, 0)

    qs = mm(half, qp[6])
    qs = jnp.concatenate([qs, jnp.zeros((64, LANES), F32)], axis=0)
    shape = (LANES, LANES)
    row, col = iota(shape, 0), iota(shape, 1)
    down = jnp.where((row >= 64) & (shr(col, 1) == row - 64), 0.5, 0.0).astype(BF16)
    qs = qs.astype(BF16)
    upper_rows = iota((LANES, 1), 0) >= 64
    for _ in range(4):
        qs = jnp.where(upper_rows, mm(down, qs), qs.astype(F32)).astype(BF16)
    level = row_level(jnp.bitwise_and(iota((256, 1), 0), 127))

    for copy in stage_b:
        copy.wait_recv()
    far4 = r4[pl.ds(2 * (1 - y_pair), 2)].reshape(LANES, 256)
    far = jnp.concatenate([far4, rf[...].reshape(512, 256)], axis=0)
    far_vals = with_ones(far[:, LANES:])
    q_stack = stack_heads(qs)
    weights_s, peak_s = soft_weights(pick(mm_nt(q_stack, far[:, :LANES]), level))
    blocks_s = blocks_of(weights_s, level)
    both = mm(blocks_s, far_vals)
    weighted_s = fold(both[:, :LANES], LANES)
    total_s = fold(both[:, LANES:], LANES)
    peak_s = fold(jnp.broadcast_to(peak_s, (256, LANES)), LANES)

    spreads = level_spread()
    stats = jnp.concatenate(
        [peak_s.astype(BF16), *split2(weighted_s), *split2(total_s)], axis=1
    )
    taken = [mm(part.astype(BF16), stats) for part in spreads]
    m3 = w1p[6]
    for t in taken:
        m3 = jnp.maximum(m3, t[:, :LANES])
    a3 = jnp.exp(w1p[6] - m3)
    n3, d3 = a3 * w1w[6], a3 * w1t[6]
    shares_s = []
    for index, t in enumerate(taken):
        share = 2.0 ** (index + 1) * jnp.exp(t[:, :LANES] - m3)
        n3 = n3 + share * (t[:, 128:256] + t[:, 256:384])
        d3 = d3 + share * (t[:, 384:512] + t[:, 512:640])
        shares_s.append(share)

    def doubled(ref, values, count):
        ref[pl.ds(0, count, 2), :] = values
        ref[pl.ds(1, count, 2), :] = values
        return ref[0 : 2 * count, :]

    def paired(ref, values, count):
        ref[0:count, :] = values
        return ref[pl.ds(0, count // 2, 2), :] + ref[pl.ds(1, count // 2, 2), :]

    def merge(peak, weighted, total, m, n, d):
        crest = jnp.maximum(peak, m)
        own = jnp.exp(peak - crest)
        rest = 2.0 * jnp.exp(m - crest)
        return crest, own * weighted + rest * n, own * total + rest * d, own, rest

    m2, n2, d2, own2, rest2 = merge(
        w1p[4:6].reshape(256, LANES), w1w[4:6].reshape(256, LANES), w1t[4:6].reshape(256, LANES),
        doubled(spm, m3, 128), doubled(spn, n3, 128), doubled(spd, d3, 128),
    )
    crest1, n1v, d1v, own1, rest1 = merge(
        w1p[0:4].reshape(512, LANES), w1w[0:4].reshape(512, LANES), w1t[0:4].reshape(512, LANES),
        doubled(spm, m2, 256), doubled(spn, n2, 256), doubled(spd, d2, 256),
    )
    m1[...] = crest1.reshape(4, LANES, LANES)
    n1[...] = n1v.reshape(4, LANES, LANES)
    d1[...] = d1v.reshape(4, LANES, LANES)
    a1[...], b1[...] = own1, rest1

    same = jnp.where(shr(iota(shape, 0), 6) == shr(iota(shape, 1), 6), 1.0, 0.0).astype(BF16)
    head_sum = jnp.concatenate([same, same], axis=0)

    def output_copy(kind, mask):
        px = flip(x, mask, 2)
        if kind == 0:
            src, dst = ob.at[px], out_ref.at[:, lanes(x)]
        elif kind == 1:
            src, dst = oq.at[px], gq_ref.at[:, lanes(x)]
        else:
            src, dst = bk.at[px], bkr.at[x]
        return remote(
            src, dst, o_send.at[kind, mask - 1], o_recv.at[kind, mask - 1], place(px, y, w)
        )

    def merge_step(mask, carry):
        px = flip(x, mask, 2)

        @pl.when(mask < 4)
        def _():
            token_copies(mask)[3].wait_recv()

        crest, numer, denom, own, rest = merge(
            w0p[px], w0w[px], w0t[px],
            doubled(spm, m1[px], 128), doubled(spn, n1[px], 128), doubled(spd, d1[px], 128),
        )
        ratio = numer / denom
        ob[px] = ratio.astype(BF16)
        up = gb[px].astype(F32)
        high, low = split2(up * ratio)
        inverse = 1.0 / denom
        drift = -mm(jnp.concatenate([high, low], axis=1), head_sum) * inverse
        scaled = up * inverse
        gw0[px] = (own * scaled).astype(BF16)
        gt0[px] = own * drift
        g1s[px] = paired(spm, rest * scaled, 256)
        d1s[px] = paired(spn, rest * drift, 256)

        @pl.when(mask < 4)
        def _():
            output_copy(0, mask).start()

        return carry

    lax.fori_loop(1, 5, merge_step, 0)
    local_out = pltpu.make_async_copy(ob.at[x], out_ref.at[:, lanes(x)], loc.at[0])
    local_out.start()

    g1, dd1 = g1s[...].reshape(512, LANES), d1s[...].reshape(512, LANES)
    gw1[0:4] = (a1[...] * g1).astype(BF16).reshape(4, LANES, LANES)
    gt1[0:4] = (a1[...] * dd1).reshape(4, LANES, LANES)
    g2 = paired(g2s, b1[...] * g1, 512)
    dd2 = paired(d2s, b1[...] * dd1, 512)
    gw1[4:6] = (own2 * g2).astype(BF16).reshape(2, LANES, LANES)
    gt1[4:6] = (own2 * dd2).reshape(2, LANES, LANES)
    g3 = paired(spm, rest2 * g2, 256)
    dd3 = paired(spn, rest2 * dd2, 256)
    gw1[6] = (a3 * g3).astype(BF16)
    gt1[6] = a3 * dd3
    pieces = []
    for share in shares_s:
        pieces.append(
            jnp.concatenate([(share * g3).astype(BF16), *split2(share * dd3)], axis=1)
        )
    pooled = mm(level_pool(), jnp.concatenate(pieces, axis=0))
    gw_s = pooled[:, :LANES].astype(BF16)
    gt_s = pooled[:, 128:256] + pooled[:, 256:384]

    grads_s = stack_grads(gw_s, gt_s)
    lift = pick(mm_nt(grads_s, far_vals), level)
    gs = (weights_s.astype(F32) * lift).astype(BF16)
    gs_blocks = blocks_of(gs, level)
    gk_far = mm_tn(gs_blocks, q_stack)
    gv_far = mm_tn(blocks_s, grads_s[:, :LANES])
    far_grads = jnp.concatenate([gk_far, gv_far], axis=1)
    g4s[...] = far_grads[:LANES].reshape(2, 64, 256)
    sb[...] = far_grads[LANES:].astype(BF16).reshape(32, 16, 256)

    back_b = []
    for m in range(1, 16):
        up = m.bit_length() - 1
        count = 8 >> up
        pw = flip(w, m, 4)
        theirs = 8 * up + (pw % 2**up) * count
        ours = 8 * up + (w % 2**up) * count
        copy = remote(
            sb.at[pl.ds(theirs, count)], rb.at[pl.ds(ours, count)],
            bb_send.at[m - 1], bb_recv.at[m - 1], place(x, y, pw),
        )
        copy.start()
        back_b.append(copy)

    gq_s = fold(mm(gs_blocks, far[:, :LANES]), LANES) * 0.125
    high, low = split2(gq_s)
    weighted_spread = spreads[0] * 0.5
    for index in range(1, 5):
        weighted_spread = weighted_spread + spreads[index] * 0.5 ** (index + 1)
    weighted_spread = weighted_spread.astype(BF16)
    run_q3 = mm(weighted_spread, high) + mm(weighted_spread, low)

    def unit_back(index, carry):
        unit = 6 - index
        other = unit + 1 - 2 * (unit % 2)
        gq, gkv = attend_back(qp[unit], kvp[other], w1[unit], gw1[unit], gt1[unit])
        gq1[unit] = gq
        gkv1[other] = gkv
        return carry

    lax.fori_loop(0, 7, unit_back, 0)

    run_q2 = gq1[4:6].reshape(256, LANES) + 0.5 * doubled(spm, gq1[6] + run_q3, 128)
    run_q1 = gq1[0:4].reshape(512, LANES) + 0.5 * doubled(spm, run_q2, 256)
    run_k2 = gkv1[4:6, :, :LANES].reshape(256, LANES)
    run_v2 = gkv1[4:6, :, LANES:].reshape(256, LANES)
    run_k1 = gkv1[0:4, :, :LANES].reshape(512, LANES) + 0.5 * doubled(spn, run_k2, 256)
    run_v1 = gkv1[0:4, :, LANES:].reshape(512, LANES) + 0.5 * doubled(spd, run_v2, 256)
    m1[...] = run_q1.reshape(4, LANES, LANES)
    n1[...] = run_k1.reshape(4, LANES, LANES)
    d1[...] = run_v1.reshape(4, LANES, LANES)

    def chunk_back(mask, carry):
        px = flip(x, mask, 2)
        gq, gkv = attend_back(qb[px], kvb[px], w0[px], gw0[px], gt0[px])
        oq[px] = (gq + 0.5 * doubled(spm, m1[px], 128)).astype(BF16)
        bk[px, :, :LANES] = (gkv[:, :LANES] + 0.5 * doubled(spn, n1[px], 128)).astype(BF16)
        bk[px, :, LANES:] = (gkv[:, LANES:] + 0.5 * doubled(spd, d1[px], 128)).astype(BF16)

        @pl.when(mask < 4)
        def _():
            output_copy(1, mask).start()
            output_copy(2, mask).start()

        return carry

    lax.fori_loop(1, 5, chunk_back, 0)
    local_q = pltpu.make_async_copy(oq.at[x], gq_ref.at[:, lanes(x)], loc.at[1])
    local_q.start()

    for copy in back_b:
        copy.wait_recv()
    shape = (LANES, LANES)
    row, col = iota(shape, 0), iota(shape, 1)
    gather = []
    for up in range(4):
        inside = jnp.bitwise_and(col, (LANES >> up) - 1)
        gather.append(jnp.where(shr(row, up) == inside, 0.5**up, 0.0))
    gather = jnp.concatenate(gather, axis=1).astype(BF16)
    run5 = mm(gather, rb[...].reshape(512, 256)).astype(BF16)
    t4[...] = mm(spread_matrix(LANES, 0.5), run5).reshape(4, 64, 256)
    m4s[y] = t4[y].astype(BF16).reshape(4, 16, 256)
    other_pair = 2 * (1 - y_pair)
    for half_index in range(2):
        slot = other_pair + half_index
        m4s[slot] = (t4[slot] + g4s[half_index]).astype(BF16).reshape(4, 16, 256)
    near = mm(spread_matrix(64, 0.5), t4[sib].astype(BF16)) + gkv1[7]
    m3s[...] = near.astype(BF16).reshape(4, 2, 16, 256)

    back_a = []
    for index, (mx, my) in enumerate(plane):
        px, py = flip(x, mx, 2), flip(y, my, 2)
        if my == 0:
            src, dst = m4s.at[py, pl.ds(px, 1)], cb.at[x, pl.ds(0, 1)]
        elif my == 1:
            src, dst = m3s.at[px], cb.at[x, pl.ds(1, 2)]
        else:
            src, dst = m4s.at[py, pl.ds(px, 1)], cb.at[x, pl.ds(3 + y_bit, 1)]
        copy = remote(src, dst, aa_send.at[index], aa_recv.at[index], place(px, py, w))
        copy.start()
        back_a.append(copy)
    cb[x, 0] = m4s[y, x]
    bkr[x] = bk[x]

    for mask in (1, 2, 3):
        for kind in range(3):
            output_copy(kind, mask).wait_recv()
    shape = (256, 80)
    token, unit = iota(shape, 0), iota(shape, 1)
    fine = (unit >= 16) & (unit < 48) & (shr(token, 3) == unit - 16)
    coarse = ((unit < 16) | (unit >= 48)) & (shr(token, 4) == jnp.bitwise_and(unit, 15))
    last = (jnp.where(fine, 0.125, 0.0) + jnp.where(coarse, 0.0625, 0.0)).astype(BF16)
    for copy in back_a:
        copy.wait_recv()
    for j in range(4):
        total = mm(last, cb[j].reshape(80, 256)) + bkr[j].astype(F32)
        gk_ref[:, j * LANES : (j + 1) * LANES] = total[:, :LANES].astype(BF16)
        gv_ref[:, j * LANES : (j + 1) * LANES] = total[:, LANES:].astype(BF16)

    local_out.wait()
    local_q.wait()
    for copies in (stage_a, stage_b, back_b, back_a):
        for copy in copies:
            copy.wait_send()
    for mask in (1, 2, 3):
        for copy in token_copies(mask):
            copy.wait_send()
        for kind in range(3):
            output_copy(kind, mask).wait_send()


def shards(query, key_in, value_in, grad_out):
    rows, width = query.shape
    whole = jax.ShapeDtypeStruct((rows, width), BF16)

    def f32(*shape):
        return pltpu.VMEM(shape, F32)

    def b16(*shape):
        return pltpu.VMEM(shape, BF16)

    dma = pltpu.SemaphoreType.DMA
    scratch = [
        b16(4, 256, 128), b16(4, 256, 256), b16(4, 256, 128),
        b16(4, 32, 256), b16(4, 16, 256),
        b16(4, 32, 256), b16(4, 32, 256), b16(4, 4, 16, 256),
        b16(8, 16, 256), b16(4, 16, 256), b16(2, 16, 256), b16(1, 16, 256),
        b16(32, 16, 256),
        b16(7, 128, 128), b16(8, 128, 256),
        b16(4, 512, 256), b16(7, 256, 128),
        f32(4, 256, 128), f32(4, 256, 128), f32(4, 256, 128),
        f32(7, 128, 128), f32(7, 128, 128), f32(7, 128, 128),
        f32(512, 128), f32(512, 128),
        f32(4, 128, 128), f32(4, 128, 128), f32(4, 128, 128),
        b16(4, 256, 128), f32(4, 256, 128), b16(7, 128, 128), f32(7, 128, 128),
        f32(512, 128), f32(512, 128), f32(512, 128),
        f32(4, 128, 128), f32(4, 128, 128), f32(512, 128), f32(512, 128),
        b16(4, 256, 128), b16(4, 256, 128), b16(4, 256, 256), b16(4, 256, 256),
        f32(7, 128, 128), f32(8, 128, 256), f32(8, 128),
        b16(32, 16, 256), b16(32, 16, 256),
        f32(4, 64, 256), b16(4, 2, 16, 256), b16(4, 4, 16, 256),
        b16(4, 5, 16, 256), f32(2, 64, 256),
        dma((4, 3)), dma((4, 3)), dma((15,)), dma((15,)), dma((15,)), dma((15,)),
        dma((15,)), dma((15,)), dma((15,)), dma((15,)), dma((3, 3)), dma((3, 3)), dma((2,)),
    ]
    vmem = pl.BlockSpec(memory_space=pltpu.VMEM)
    anywhere = pl.BlockSpec(memory_space=pl.ANY)
    return pl.pallas_call(
        kernel,
        out_shape=(whole, whole, whole, whole),
        in_specs=[vmem] * 4,
        out_specs=(anywhere, anywhere, vmem, vmem),
        scratch_shapes=scratch,
        compiler_params=pltpu.CompilerParams(
            collective_id=0, has_side_effects=True, vmem_limit_bytes=40 * 2**20
        ),
    )(query, key_in, value_in, grad_out)


def solution(mesh):
    spec = P(("grp", "seq"), None)
    return jax.shard_map(
        shards, mesh=mesh, in_specs=(spec,) * 4, out_specs=(spec,) * 4, check_vma=False
    )
```

profile of v0, /device:TPU:6, one launch (start us, length us, event | category | flops | bytes accessed | tf_op | source)
XLA Modules:
  0.0 59.0 jit_solution(14425582362508093040)
XLA Ops:
  0.6 0.0 copy-start
  0.6 0.9 %copy-done = bf16[256,512]{1,0:T(8,128)(2,1)S(1)} copy-done((bf16[256,512]{1,0:T(8,128)(2,1)S(1)}, bf16[256,512]{1,0:T(8,128)(2,1)}, u32[]{:S(2)}) %copy-start) | copy-done | bytes 262168
  1.6 0.0 copy-start.1
  1.6 0.9 %copy-done.1 = bf16[256,512]{1,0:T(8,128)(2,1)S(1)} copy-done((bf16[256,512]{1,0:T(8,128)(2,1)S(1)}, bf16[256,512]{1,0:T(8,128)(2,1)}, u32[]{:S(2)}) %copy-start.1) | copy-done | bytes 262168
  2.5 0.0 copy-start.2
  2.5 0.9 %copy-done.2 = bf16[256,512]{1,0:T(8,128)(2,1)S(1)} copy-done((bf16[256,512]{1,0:T(8,128)(2,1)S(1)}, bf16[256,512]{1,0:T(8,128)(2,1)}, u32[]{:S(2)}) %copy-start.2) | copy-done | bytes 262168
  3.5 0.0 copy-start.3
  3.5 0.9 %copy-done.3 = bf16[256,512]{1,0:T(8,128)(2,1)S(1)} copy-done((bf16[256,512]{1,0:T(8,128)(2,1)S(1)}, bf16[256,512]{1,0:T(8,128)(2,1)}, u32[]{:S(2)}) %copy-start.3) | copy-done | bytes 262168
  4.4 51.8 %shard_map.75 = (bf16[256,512]{1,0:T(8,128)(2,1)S(1)}, bf16[256,512]{1,0:T(8,128)(2,1)S(1)}, bf16[256,512]{1,0:T(8,128)(2,1)S(1)}, bf16[256,512]{1,0:T(8,128)(2,1)S(1)}) custom-call(bf16[256,512]{1,0:T(8,128)(2,1)S(1)} %copy-done, bf16[256,512]{1,0:T(8,128)(2,1)S(1)} %copy-done.1, bf16[256,512]{1,0:T(8,128)(2,1)S(1)} %copy-done.2, bf16[256,512]{1,0:T(8,128)(2,1)S(1)} %copy-done.3), custom_call_target="tpu_custom_call" | custom-call | tf_op jit(solution)/shard_map/pallas_call | solution.py:630
  56.2 0.7 %copy.12 = bf16[256,512]{1,0:T(8,128)(2,1)} copy(bf16[256,512]{1,0:T(8,128)(2,1)S(1)} %get-tuple-element.8) | data formatting | bytes 524288
  56.9 0.7 %copy.13 = bf16[256,512]{1,0:T(8,128)(2,1)} copy(bf16[256,512]{1,0:T(8,128)(2,1)S(1)} %get-tuple-element.9) | data formatting | bytes 524288
  57.6 0.7 %copy.14 = bf16[256,512]{1,0:T(8,128)(2,1)} copy(bf16[256,512]{1,0:T(8,128)(2,1)S(1)} %get-tuple-element.10) | data formatting | bytes 524288
  58.3 0.7 %copy.15 = bf16[256,512]{1,0:T(8,128)(2,1)} copy(bf16[256,512]{1,0:T(8,128)(2,1)S(1)} %get-tuple-element.11) | data formatting | bytes 524288
Async XLA Ops:
  0.6 1.0 %copy-start = (bf16[256,512]{1,0:T(8,128)(2,1)S(1)}, bf16[256,512]{1,0:T(8,128)(2,1)}, u32[]{:S(2)}) copy-start(bf16[256,512]{1,0:T(8,128)(2,1)} %q_ref.1) | copy-start | bytes 786436
  1.6 0.9 %copy-start.1 = (bf16[256,512]{1,0:T(8,128)(2,1)S(1)}, bf16[256,512]{1,0:T(8,128)(2,1)}, u32[]{:S(2)}) copy-start(bf16[256,512]{1,0:T(8,128)(2,1)} %k_ref.1) | copy-start | bytes 786436
  2.5 0.9 %copy-start.2 = (bf16[256,512]{1,0:T(8,128)(2,1)S(1)}, bf16[256,512]{1,0:T(8,128)(2,1)}, u32[]{:S(2)}) copy-start(bf16[256,512]{1,0:T(8,128)(2,1)} %v_ref.1) | copy-start | bytes 786436
  3.5 0.9 %copy-start.3 = (bf16[256,512]{1,0:T(8,128)(2,1)S(1)}, bf16[256,512]{1,0:T(8,128)(2,1)}, u32[]{:S(2)}) copy-start(bf16[256,512]{1,0:T(8,128)(2,1)} %g_ref.1) | copy-start | bytes 786436
where the time goes:
time: 59.4 us; the launch traced here: 59 us
  Pallas kernels  51.8 us (87%)
  local copies, waits for them, and re-layouts  6.6 us (11%)
  between operations  0.65 us (1%)
    pallas_call x1, Pallas kernels, shards(): pl.pallas_call(kernel, out_shape=(whole, whole, whole, whole), in_specs=[...  51.8 us
    unnamed x12, local copies, waits for them, and re-layouts  6.6 us

commit v1 on v0

--- a/solution.py
+++ b/solution.py
@@ -174,13 +174,13 @@
 
 
 def kernel(
-    q_ref, k_ref, v_ref, g_ref, out_ref, gq_ref, gk_ref, gv_ref,
-    qb, kvb, gb, l3, l4, kv3own, kv3sib, r4, own5, own6, own7, own8, rf,
+    q_hbm, k_hbm, v_hbm, g_hbm, out_ref, gq_ref, cb, bkr,
+    q_ref, k_ref, v_ref, g_ref, qb, kvb, gb, l3, l4, kv3sib, r4, own5, own6, own7, own8, rf,
     qp, kvp, w0, w1, w0w, w0p, w0t, w1w, w1p, w1t,
-    a1, b1, m1, n1, d1, gw0, gt0, gw1, gt1, spm, spn, spd, g1s, d1s, g2s, d2s,
-    ob, oq, bk, bkr, gq1, gkv1, gkv2, sb, rb, t4, m3s, m4s, cb, g4s,
-    p_send, p_recv, a_send, a_recv, b_send, b_recv, bb_send, bb_recv, aa_send, aa_recv,
-    o_send, o_recv, loc,
+    m1, n1, d1, gw0, gt0, gw1, gt1, sp, g1s, d1s,
+    ob, oq, bk, gq1, gkv1, sb, rb, t4, m3s, m4s, g4s,
+    p_send, p_recv, a_send, a_recv, c_send, c_recv, b_send, b_recv, bb_send, bb_recv,
+    aa_send, aa_recv, o_send, o_recv, loc,
 ):
     grp, seq = lax.axis_index("grp"), lax.axis_index("seq")
     x, y = seq % 4, (seq // 4) % 4
@@ -209,25 +209,32 @@
             barrier, inc=1, device_id=place(x, y, flip(w, m, 4)), device_id_type=MESH
         )
 
+    loads = []
+    for index, (src, dst) in enumerate(
+        ((k_hbm, k_ref), (v_hbm, v_ref), (q_hbm, q_ref), (g_hbm, g_ref))
+    ):
+        copy = pltpu.make_async_copy(src, dst, loc.at[index])
+        copy.start()
+        loads.append(copy)
+
     for part, ref in ((0, k_ref), (1, v_ref)):
+        loads[part].wait()
         rows = coarsen(coarsen(coarsen(ref[...])))
         upper = coarsen(rows)
         for j in range(4):
             l3[j, :, part * LANES : (part + 1) * LANES] = rows[:, j * LANES : (j + 1) * LANES]
             l4[j, :, part * LANES : (part + 1) * LANES] = upper[:, j * LANES : (j + 1) * LANES]
 
+    loads[2].wait()
+    loads[3].wait()
     pl.semaphore_wait(barrier, 30)
 
     stage_a = []
     for index, (mx, my) in enumerate(plane):
         px, py = flip(x, mx, 2), flip(y, my, 2)
-        if my == 0:
-            src, dst = l3.at[px], kv3own.at[x]
-        elif my == 1:
-            src, dst = l3.at[px], kv3sib.at[x]
-        else:
-            src, dst = l4.at[px], r4.at[y, x]
-        copy = remote(src, dst, a_send.at[index], a_recv.at[index], place(px, py, w))
+        copy = remote(
+            l4.at[px], r4.at[y, x], a_send.at[index], a_recv.at[index], place(px, py, w)
+        )
         copy.start()
         stage_a.append(copy)
 
@@ -250,16 +257,26 @@
             for i, (ref, dst) in enumerate(pairs)
         ]
 
-    moves = [token_copies(mask) for mask in (1, 2, 3)]
-    for i in range(4):
-        for copies in moves:
-            copies[i].start()
+    moves = {mask: token_copies(mask) for mask in (1, 2, 3)}
+    for i in range(3):
+        moves[1][i].start()
+        moves[3][i].start()
+    stage_c = []
+    for mx in range(4):
+        px = flip(x, mx, 2)
+        copy = remote(l3.at[px], kv3sib.at[x], c_send.at[mx], c_recv.at[mx], place(px, sib, w))
+        copy.start()
+        stage_c.append(copy)
+    for i in range(3):
+        moves[2][i].start()
+    for mask in (1, 3, 2):
+        moves[mask][3].start()
 
     kvb[x, :, :LANES] = k_ref[:, lanes(x)]
     kvb[x, :, LANES:] = v_ref[:, lanes(x)]
     qb[x] = q_ref[:, lanes(x)]
     gb[x] = g_ref[:, lanes(x)]
-    kv3own[x] = l3[x]
+    r4[y, x] = l4[x]
 
     def chunk_forward(slot):
         q, kv = qb[slot], kvb[slot]
@@ -274,9 +291,6 @@
     for copy in stage_a:
         copy.wait_recv()
     half = pool_matrix(LANES)
-    r4[y] = mm(half, kv3own[...].reshape(LANES, 256)).astype(BF16).reshape(4, 16, 256)
-    r4[sib] = mm(half, kv3sib[...].reshape(LANES, 256)).astype(BF16).reshape(4, 16, 256)
-    kvp[7] = kv3sib[...].reshape(LANES, 256)
     rows5 = coarsen(r4[...].reshape(256, 256))
     rows6 = coarsen(rows5)
     rows7 = coarsen(rows6)
@@ -299,29 +313,30 @@
         copy.start()
         stage_b.append(copy)
 
-    def chunk_step(mask, carry):
-        px = flip(x, mask, 2)
-        for copy in token_copies(mask)[:3]:
+    def unit_forward(unit, other):
+        weights, peak, weighted, total = attend(qp[unit], kvp[other])
+        w1[unit] = weights
+        w1p[unit], w1w[unit], w1t[unit] = peak, weighted, total
+
+    for mask in (1, 3, 2):
+        for copy in moves[mask][:3]:
             copy.wait_recv()
-        chunk_forward(px)
-        return carry
-
-    lax.fori_loop(1, 4, chunk_step, 0)
-
+        chunk_forward(flip(x, mask, 2))
+        if mask == 1:
+            unit_forward(x, flip(x, 1, 2))
+            unit_forward(flip(x, 1, 2), x)
+    unit_forward(flip(x, 3, 2), flip(x, 2, 2))
+    unit_forward(flip(x, 2, 2), flip(x, 3, 2))
+    for copy in stage_c:
+        copy.wait_recv()
+    kvp[7] = kv3sib[...].reshape(LANES, 256)
     qp[4] = coarsen(qp[0:2].reshape(256, LANES))
     qp[5] = coarsen(qp[2:4].reshape(256, LANES))
     kvp[4] = coarsen(kvp[0:2].reshape(256, 256))
     kvp[5] = coarsen(kvp[2:4].reshape(256, 256))
     qp[6] = coarsen(qp[4:6].reshape(256, LANES))
-
-    def unit_step(unit, carry):
-        other = unit + 1 - 2 * (unit % 2)
-        weights, peak, weighted, total = attend(qp[unit], kvp[other])
-        w1[unit] = weights
-        w1p[unit], w1w[unit], w1t[unit] = peak, weighted, total
-        return carry
-
-    lax.fori_loop(0, 7, unit_step, 0)
+    for unit in (4, 5, 6):
+        unit_forward(unit, unit ^ 1)
 
     qs = mm(half, qp[6])
     qs = jnp.concatenate([qs, jnp.zeros((64, LANES), F32)], axis=0)
@@ -364,12 +379,20 @@
         d3 = d3 + share * (t[:, 384:512] + t[:, 512:640])
         shares_s.append(share)
 
-    def doubled(ref, values, count):
+    used = [0]
+
+    def fresh():
+        used[0] += 1
+        return sp.at[used[0] - 1]
+
+    def doubled(values):
+        count, ref = values.shape[0], fresh()
         ref[pl.ds(0, count, 2), :] = values
         ref[pl.ds(1, count, 2), :] = values
         return ref[0 : 2 * count, :]
 
-    def paired(ref, values, count):
+    def paired(values):
+        count, ref = values.shape[0], fresh()
         ref[0:count, :] = values
         return ref[pl.ds(0, count // 2, 2), :] + ref[pl.ds(1, count // 2, 2), :]
 
@@ -381,16 +404,15 @@
 
     m2, n2, d2, own2, rest2 = merge(
         w1p[4:6].reshape(256, LANES), w1w[4:6].reshape(256, LANES), w1t[4:6].reshape(256, LANES),
-        doubled(spm, m3, 128), doubled(spn, n3, 128), doubled(spd, d3, 128),
+        doubled(m3), doubled(n3), doubled(d3),
     )
     crest1, n1v, d1v, own1, rest1 = merge(
         w1p[0:4].reshape(512, LANES), w1w[0:4].reshape(512, LANES), w1t[0:4].reshape(512, LANES),
-        doubled(spm, m2, 256), doubled(spn, n2, 256), doubled(spd, d2, 256),
+        doubled(m2), doubled(n2), doubled(d2),
     )
     m1[...] = crest1.reshape(4, LANES, LANES)
     n1[...] = n1v.reshape(4, LANES, LANES)
     d1[...] = d1v.reshape(4, LANES, LANES)
-    a1[...], b1[...] = own1, rest1
 
     same = jnp.where(shr(iota(shape, 0), 6) == shr(iota(shape, 1), 6), 1.0, 0.0).astype(BF16)
     head_sum = jnp.concatenate([same, same], axis=0)
@@ -407,48 +429,40 @@
             src, dst, o_send.at[kind, mask - 1], o_recv.at[kind, mask - 1], place(px, y, w)
         )
 
-    def merge_step(mask, carry):
+    for mask in (1, 3, 2):
+        moves[mask][3].wait_recv()
+    for mask in (1, 3, 2, 0):
         px = flip(x, mask, 2)
-
-        @pl.when(mask < 4)
-        def _():
-            token_copies(mask)[3].wait_recv()
-
         crest, numer, denom, own, rest = merge(
-            w0p[px], w0w[px], w0t[px],
-            doubled(spm, m1[px], 128), doubled(spn, n1[px], 128), doubled(spd, d1[px], 128),
-        )
-        ratio = numer / denom
-        ob[px] = ratio.astype(BF16)
+            w0p[px], w0w[px], w0t[px], doubled(m1[px]), doubled(n1[px]), doubled(d1[px])
+        )
+        inverse = 1.0 / denom
+        ratio = numer * inverse
         up = gb[px].astype(F32)
         high, low = split2(up * ratio)
-        inverse = 1.0 / denom
         drift = -mm(jnp.concatenate([high, low], axis=1), head_sum) * inverse
         scaled = up * inverse
+        if mask:
+            ob[px] = ratio.astype(BF16)
+        else:
+            out_ref[:, lanes(x)] = ratio.astype(BF16)
         gw0[px] = (own * scaled).astype(BF16)
         gt0[px] = own * drift
-        g1s[px] = paired(spm, rest * scaled, 256)
-        d1s[px] = paired(spn, rest * drift, 256)
-
-        @pl.when(mask < 4)
-        def _():
-            output_copy(0, mask).start()
-
-        return carry
-
-    lax.fori_loop(1, 5, merge_step, 0)
-    local_out = pltpu.make_async_copy(ob.at[x], out_ref.at[:, lanes(x)], loc.at[0])
-    local_out.start()
+        g1s[px] = paired(rest * scaled)
+        d1s[px] = paired(rest * drift)
+    outs = {(kind, mask): output_copy(kind, mask) for kind in range(3) for mask in (1, 3, 2)}
+    for mask in (1, 3, 2):
+        outs[0, mask].start()
 
     g1, dd1 = g1s[...].reshape(512, LANES), d1s[...].reshape(512, LANES)
-    gw1[0:4] = (a1[...] * g1).astype(BF16).reshape(4, LANES, LANES)
-    gt1[0:4] = (a1[...] * dd1).reshape(4, LANES, LANES)
-    g2 = paired(g2s, b1[...] * g1, 512)
-    dd2 = paired(d2s, b1[...] * dd1, 512)
+    gw1[0:4] = (own1 * g1).astype(BF16).reshape(4, LANES, LANES)
+    gt1[0:4] = (own1 * dd1).reshape(4, LANES, LANES)
+    g2 = paired(rest1 * g1)
+    dd2 = paired(rest1 * dd1)
     gw1[4:6] = (own2 * g2).astype(BF16).reshape(2, LANES, LANES)
     gt1[4:6] = (own2 * dd2).reshape(2, LANES, LANES)
-    g3 = paired(spm, rest2 * g2, 256)
-    dd3 = paired(spn, rest2 * dd2, 256)
+    g3 = paired(rest2 * g2)
+    dd3 = paired(rest2 * dd2)
     gw1[6] = (a3 * g3).astype(BF16)
     gt1[6] = a3 * dd3
     pieces = []
@@ -492,43 +506,37 @@
     weighted_spread = weighted_spread.astype(BF16)
     run_q3 = mm(weighted_spread, high) + mm(weighted_spread, low)
 
-    def unit_back(index, carry):
-        unit = 6 - index
-        other = unit + 1 - 2 * (unit % 2)
-        gq, gkv = attend_back(qp[unit], kvp[other], w1[unit], gw1[unit], gt1[unit])
-        gq1[unit] = gq
-        gkv1[other] = gkv
-        return carry
-
-    lax.fori_loop(0, 7, unit_back, 0)
-
-    run_q2 = gq1[4:6].reshape(256, LANES) + 0.5 * doubled(spm, gq1[6] + run_q3, 128)
-    run_q1 = gq1[0:4].reshape(512, LANES) + 0.5 * doubled(spm, run_q2, 256)
+    for unit in range(6, -1, -1):
+        gq1[unit], gkv1[unit ^ 1] = attend_back(
+            qp[unit], kvp[unit ^ 1], w1[unit], gw1[unit], gt1[unit]
+        )
+
+    run_q2 = gq1[4:6].reshape(256, LANES) + 0.5 * doubled(gq1[6] + run_q3)
+    run_q1 = gq1[0:4].reshape(512, LANES) + 0.5 * doubled(run_q2)
     run_k2 = gkv1[4:6, :, :LANES].reshape(256, LANES)
     run_v2 = gkv1[4:6, :, LANES:].reshape(256, LANES)
-    run_k1 = gkv1[0:4, :, :LANES].reshape(512, LANES) + 0.5 * doubled(spn, run_k2, 256)
-    run_v1 = gkv1[0:4, :, LANES:].reshape(512, LANES) + 0.5 * doubled(spd, run_v2, 256)
+    run_k1 = gkv1[0:4, :, :LANES].reshape(512, LANES) + 0.5 * doubled(run_k2)
+    run_v1 = gkv1[0:4, :, LANES:].reshape(512, LANES) + 0.5 * doubled(run_v2)
     m1[...] = run_q1.reshape(4, LANES, LANES)
     n1[...] = run_k1.reshape(4, LANES, LANES)
     d1[...] = run_v1.reshape(4, LANES, LANES)
 
-    def chunk_back(mask, carry):
+    for mask in (1, 3, 2, 0):
         px = flip(x, mask, 2)
         gq, gkv = attend_back(qb[px], kvb[px], w0[px], gw0[px], gt0[px])
-        oq[px] = (gq + 0.5 * doubled(spm, m1[px], 128)).astype(BF16)
-        bk[px, :, :LANES] = (gkv[:, :LANES] + 0.5 * doubled(spn, n1[px], 128)).astype(BF16)
-        bk[px, :, LANES:] = (gkv[:, LANES:] + 0.5 * doubled(spd, d1[px], 128)).astype(BF16)
-
-        @pl.when(mask < 4)
-        def _():
-            output_copy(1, mask).start()
-            output_copy(2, mask).start()
-
-        return carry
-
-    lax.fori_loop(1, 5, chunk_back, 0)
-    local_q = pltpu.make_async_copy(oq.at[x], gq_ref.at[:, lanes(x)], loc.at[1])
-    local_q.start()
+        gq = (gq + 0.5 * doubled(m1[px])).astype(BF16)
+        gk = (gkv[:, :LANES] + 0.5 * doubled(n1[px])).astype(BF16)
+        gv = (gkv[:, LANES:] + 0.5 * doubled(d1[px])).astype(BF16)
+        if mask:
+            oq[px] = gq
+            bk[px, :, :LANES] = gk
+            bk[px, :, LANES:] = gv
+            outs[1, mask].start()
+            outs[2, mask].start()
+        else:
+            gq_ref[:, lanes(x)] = gq
+            bkr[x, :, :LANES] = gk
+            bkr[x, :, LANES:] = gv
 
     for copy in back_b:
         copy.wait_recv()
@@ -562,33 +570,36 @@
         copy.start()
         back_a.append(copy)
     cb[x, 0] = m4s[y, x]
-    bkr[x] = bk[x]
-
-    for mask in (1, 2, 3):
-        for kind in range(3):
-            output_copy(kind, mask).wait_recv()
+
+    for copy in back_a:
+        copy.wait_recv()
+    for copy in outs.values():
+        copy.wait_recv()
+    for copies in (stage_a, stage_b, stage_c, back_b, back_a, outs.values(), *moves.values()):
+        for copy in copies:
+            copy.wait_send()
+
+
+def finish(out_v, gq_v, cb, bkr, out_ref, gq_ref, gk_ref, gv_ref, gk_v, gv_v, sems):
+    first = pltpu.make_async_copy(out_v, out_ref, sems.at[0])
+    second = pltpu.make_async_copy(gq_v, gq_ref, sems.at[1])
+    first.start()
+    second.start()
     shape = (256, 80)
     token, unit = iota(shape, 0), iota(shape, 1)
     fine = (unit >= 16) & (unit < 48) & (shr(token, 3) == unit - 16)
     coarse = ((unit < 16) | (unit >= 48)) & (shr(token, 4) == jnp.bitwise_and(unit, 15))
     last = (jnp.where(fine, 0.125, 0.0) + jnp.where(coarse, 0.0625, 0.0)).astype(BF16)
-    for copy in back_a:
-        copy.wait_recv()
     for j in range(4):
         total = mm(last, cb[j].reshape(80, 256)) + bkr[j].astype(F32)
-        gk_ref[:, j * LANES : (j + 1) * LANES] = total[:, :LANES].astype(BF16)
-        gv_ref[:, j * LANES : (j + 1) * LANES] = total[:, LANES:].astype(BF16)
-
-    local_out.wait()
-    local_q.wait()
-    for copies in (stage_a, stage_b, back_b, back_a):
-        for copy in copies:
-            copy.wait_send()
-    for mask in (1, 2, 3):
-        for copy in token_copies(mask):
-            copy.wait_send()
-        for kind in range(3):
-            output_copy(kind, mask).wait_send()
+        gk_v[:, j * LANES : (j + 1) * LANES] = total[:, :LANES].astype(BF16)
+        gv_v[:, j * LANES : (j + 1) * LANES] = total[:, LANES:].astype(BF16)
+    third = pltpu.make_async_copy(gk_v, gk_ref, sems.at[2])
+    fourth = pltpu.make_async_copy(gv_v, gv_ref, sems.at[3])
+    third.start()
+    fourth.start()
+    for copy in (first, second, third, fourth):
+        copy.wait()
 
 
 def shards(query, key_in, value_in, grad_out):
@@ -603,40 +614,49 @@
 
     dma = pltpu.SemaphoreType.DMA
     scratch = [
+        b16(256, 512), b16(256, 512), b16(256, 512), b16(256, 512),
         b16(4, 256, 128), b16(4, 256, 256), b16(4, 256, 128),
-        b16(4, 32, 256), b16(4, 16, 256),
-        b16(4, 32, 256), b16(4, 32, 256), b16(4, 4, 16, 256),
+        b16(4, 32, 256), b16(4, 16, 256), b16(4, 32, 256), b16(4, 4, 16, 256),
         b16(8, 16, 256), b16(4, 16, 256), b16(2, 16, 256), b16(1, 16, 256),
         b16(32, 16, 256),
         b16(7, 128, 128), b16(8, 128, 256),
         b16(4, 512, 256), b16(7, 256, 128),
         f32(4, 256, 128), f32(4, 256, 128), f32(4, 256, 128),
         f32(7, 128, 128), f32(7, 128, 128), f32(7, 128, 128),
-        f32(512, 128), f32(512, 128),
         f32(4, 128, 128), f32(4, 128, 128), f32(4, 128, 128),
         b16(4, 256, 128), f32(4, 256, 128), b16(7, 128, 128), f32(7, 128, 128),
-        f32(512, 128), f32(512, 128), f32(512, 128),
-        f32(4, 128, 128), f32(4, 128, 128), f32(512, 128), f32(512, 128),
-        b16(4, 256, 128), b16(4, 256, 128), b16(4, 256, 256), b16(4, 256, 256),
-        f32(7, 128, 128), f32(8, 128, 256), f32(8, 128),
+        f32(48, 512, 128), f32(4, 128, 128), f32(4, 128, 128),
+        b16(4, 256, 128), b16(4, 256, 128), b16(4, 256, 256),
+        f32(7, 128, 128), f32(8, 128, 256),
         b16(32, 16, 256), b16(32, 16, 256),
-        f32(4, 64, 256), b16(4, 2, 16, 256), b16(4, 4, 16, 256),
-        b16(4, 5, 16, 256), f32(2, 64, 256),
-        dma((4, 3)), dma((4, 3)), dma((15,)), dma((15,)), dma((15,)), dma((15,)),
-        dma((15,)), dma((15,)), dma((15,)), dma((15,)), dma((3, 3)), dma((3, 3)), dma((2,)),
+        f32(4, 64, 256), b16(4, 2, 16, 256), b16(4, 4, 16, 256), f32(2, 64, 256),
+        dma((4, 3)), dma((4, 3)), dma((15,)), dma((15,)), dma((4,)), dma((4,)),
+        dma((15,)), dma((15,)), dma((15,)), dma((15,)), dma((15,)), dma((15,)),
+        dma((3, 3)), dma((3, 3)), dma((4,)),
     ]
     vmem = pl.BlockSpec(memory_space=pltpu.VMEM)
-    anywhere = pl.BlockSpec(memory_space=pl.ANY)
-    return pl.pallas_call(
+    hbm = pl.BlockSpec(memory_space=pltpu.HBM)
+    parts = pl.pallas_call(
         kernel,
-        out_shape=(whole, whole, whole, whole),
-        in_specs=[vmem] * 4,
-        out_specs=(anywhere, anywhere, vmem, vmem),
+        out_shape=(
+            whole, whole,
+            jax.ShapeDtypeStruct((4, 5, 16, 256), BF16), jax.ShapeDtypeStruct((4, 256, 256), BF16),
+        ),
+        in_specs=[hbm] * 4,
+        out_specs=(vmem,) * 4,
         scratch_shapes=scratch,
         compiler_params=pltpu.CompilerParams(
             collective_id=0, has_side_effects=True, vmem_limit_bytes=40 * 2**20
         ),
     )(query, key_in, value_in, grad_out)
+    return pl.pallas_call(
+        finish,
+        out_shape=(whole,) * 4,
+        in_specs=[vmem] * 4,
+        out_specs=(hbm,) * 4,
+        scratch_shapes=[b16(256, 512), b16(256, 512), dma((4,))],
+        compiler_params=pltpu.CompilerParams(vmem_limit_bytes=8 * 2**20),
+    )(*parts)
 
 
 def solution(mesh):

time: 59.4 us -> 52.2 us (0.88)
  Pallas kernels: 51.8 us -> 47.2 us
  local copies, waits for them, and re-layouts: 6.6 us -> 3.79 us
    pallas_call x1 -> x2, Pallas kernels: 51.8 us -> 47.2 us  [the longest x1 46.1 us: shards(): pl.pallas_call(kernel, out_shape=(whole, whole, jax.ShapeDtypeStruct((4,...]
    unnamed x12 -> x8, local copies, waits for them, and re-layouts: 6.6 us -> 3.79 us
where the time goes in v1:
time: 52.2 us; the launch traced here: 51.6 us
  Pallas kernels  47.2 us (90%)
  local copies, waits for them, and re-layouts  3.79 us (7%)
  between operations  0.65 us (1%)
    pallas_call x1, Pallas kernels, shards(): pl.pallas_call(kernel, out_shape=(whole, whole, jax.ShapeDtypeStruct((4,...  46.1 us
    unnamed x8, local copies, waits for them, and re-layouts  3.79 us
    pallas_call x1, Pallas kernels, shards(): pl.pallas_call(finish, out_shape=(whole,) * 4, in_specs=[vmem] * 4, out_s...  1.11 us

profile of v1, /device:TPU:6, one launch (start us, length us, event | category | flops | bytes accessed | tf_op | source)
XLA Modules:
  0.0 51.6 jit_solution(4575016519843471676)
XLA Ops:
  0.6 0.0 copy-start
  0.6 0.9 %copy-done = bf16[256,512]{1,0:T(8,128)(2,1)S(1)} copy-done((bf16[256,512]{1,0:T(8,128)(2,1)S(1)}, bf16[256,512]{1,0:T(8,128)(2,1)}, u32[]{:S(2)}) %copy-start) | copy-done | bytes 262168
  1.6 0.0 copy-start.1
  1.6 0.9 %copy-done.1 = bf16[256,512]{1,0:T(8,128)(2,1)S(1)} copy-done((bf16[256,512]{1,0:T(8,128)(2,1)S(1)}, bf16[256,512]{1,0:T(8,128)(2,1)}, u32[]{:S(2)}) %copy-start.1) | copy-done | bytes 262168
  2.5 0.0 copy-start.2
  2.5 0.9 %copy-done.2 = bf16[256,512]{1,0:T(8,128)(2,1)S(1)} copy-done((bf16[256,512]{1,0:T(8,128)(2,1)S(1)}, bf16[256,512]{1,0:T(8,128)(2,1)}, u32[]{:S(2)}) %copy-start.2) | copy-done | bytes 262168
  3.5 0.0 copy-start.3
  3.5 0.9 %copy-done.3 = bf16[256,512]{1,0:T(8,128)(2,1)S(1)} copy-done((bf16[256,512]{1,0:T(8,128)(2,1)S(1)}, bf16[256,512]{1,0:T(8,128)(2,1)}, u32[]{:S(2)}) %copy-start.3) | copy-done | bytes 262168
  4.4 46.1 %shard_map.75 = (bf16[256,512]{1,0:T(8,128)(2,1)S(1)}, bf16[256,512]{1,0:T(8,128)(2,1)S(1)}, bf16[4,5,16,256]{3,2,1,0:T(8,128)(2,1)S(1)}, bf16[4,256,256]{2,1,0:T(8,128)(2,1)S(1)}) custom-call(bf16[256,512]{1,0:T(8,128)(2,1)S(1)} %copy-done, bf16[256,512]{1,0:T(8,128)(2,1)S(1)} %copy-done.1, bf16[256,512]{1,0:T(8,128)(2,1)S(1)} %copy-done.2, ...), custom_call_target="tpu_custom_call" | custom-call | tf_op jit(solution)/shard_map/pallas_call | solution.py:639
  50.5 1.1 %shard_map.76 = (bf16[256,512]{1,0:T(8,128)(2,1)}, bf16[256,512]{1,0:T(8,128)(2,1)}, bf16[256,512]{1,0:T(8,128)(2,1)}, bf16[256,512]{1,0:T(8,128)(2,1)}) custom-call(bf16[256,512]{1,0:T(8,128)(2,1)S(1)} %get-tuple-element.8.out_v, bf16[256,512]{1,0:T(8,128)(2,1)S(1)} %get-tuple-element.9.gq_v, bf16[4,5,16,256]{3,2,1,0:T(8,128)(2,1)S(1)} %get-tuple-element.10.cb, ...), custom_call_target="tpu_custom_call" | custom-call | tf_op jit(solution)/shard_map/pallas_call | solution.py:652
Async XLA Ops:
  0.6 1.0 %copy-start = (bf16[256,512]{1,0:T(8,128)(2,1)S(1)}, bf16[256,512]{1,0:T(8,128)(2,1)}, u32[]{:S(2)}) copy-start(bf16[256,512]{1,0:T(8,128)(2,1)} %q_hbm.1) | copy-start | bytes 786436
  1.6 0.9 %copy-start.1 = (bf16[256,512]{1,0:T(8,128)(2,1)S(1)}, bf16[256,512]{1,0:T(8,128)(2,1)}, u32[]{:S(2)}) copy-start(bf16[256,512]{1,0:T(8,128)(2,1)} %k_hbm.1) | copy-start | bytes 786436
  2.5 0.9 %copy-start.2 = (bf16[256,512]{1,0:T(8,128)(2,1)S(1)}, bf16[256,512]{1,0:T(8,128)(2,1)}, u32[]{:S(2)}) copy-start(bf16[256,512]{1,0:T(8,128)(2,1)} %v_hbm.1) | copy-start | bytes 786436
  3.5 0.9 %copy-start.3 = (bf16[256,512]{1,0:T(8,128)(2,1)S(1)}, bf16[256,512]{1,0:T(8,128)(2,1)}, u32[]{:S(2)}) copy-start(bf16[256,512]{1,0:T(8,128)(2,1)} %g_hbm.1) | copy-start | bytes 786436

commit v2 on v1

--- a/solution.py
+++ b/solution.py
@@ -175,12 +175,12 @@
 
 def kernel(
     q_hbm, k_hbm, v_hbm, g_hbm, out_ref, gq_ref, cb, bkr,
-    q_ref, k_ref, v_ref, g_ref, qb, kvb, gb, l3, l4, kv3sib, r4, own5, own6, own7, own8, rf,
+    k_ref, v_ref, qb, kvb, gb, l4, own3, kv3sib, r4, own5, own6, own7, own8, rf,
     qp, kvp, w0, w1, w0w, w0p, w0t, w1w, w1p, w1t,
     m1, n1, d1, gw0, gt0, gw1, gt1, sp, g1s, d1s,
-    ob, oq, bk, gq1, gkv1, sb, rb, t4, m3s, m4s, g4s,
+    ob, oq, bk, gq1, gkv1, sb, rb, s3, s4, s5, e3, e4, e5, cs, ratios, inverses,
     p_send, p_recv, a_send, a_recv, c_send, c_recv, b_send, b_recv, bb_send, bb_recv,
-    aa_send, aa_recv, o_send, o_recv, loc,
+    ey_send, ey_recv, e5_send, e5_recv, cx_send, cx_recv, o_send, o_recv, loc,
 ):
     grp, seq = lax.axis_index("grp"), lax.axis_index("seq")
     x, y = seq % 4, (seq // 4) % 4
@@ -197,9 +197,8 @@
             device_id=device, device_id_type=MESH,
         )
 
-    plane = [(mx, my) for my in (1, 2, 3, 0) for mx in range(4) if (mx, my) != (0, 0)]
-
     barrier = pltpu.get_barrier_semaphore()
+    plane = [(mx, my) for my in (2, 3, 1, 0) for mx in (2, 1, 3, 0) if (mx, my) != (0, 0)]
     for mx, my in plane:
         pl.semaphore_signal(
             barrier, inc=1, device_id=place(flip(x, mx, 2), flip(y, my, 2), w), device_id_type=MESH
@@ -209,46 +208,31 @@
             barrier, inc=1, device_id=place(x, y, flip(w, m, 4)), device_id_type=MESH
         )
 
-    loads = []
-    for index, (src, dst) in enumerate(
-        ((k_hbm, k_ref), (v_hbm, v_ref), (q_hbm, q_ref), (g_hbm, g_ref))
-    ):
-        copy = pltpu.make_async_copy(src, dst, loc.at[index])
-        copy.start()
-        loads.append(copy)
-
-    for part, ref in ((0, k_ref), (1, v_ref)):
-        loads[part].wait()
-        rows = coarsen(coarsen(coarsen(ref[...])))
-        upper = coarsen(rows)
-        for j in range(4):
-            l3[j, :, part * LANES : (part + 1) * LANES] = rows[:, j * LANES : (j + 1) * LANES]
-            l4[j, :, part * LANES : (part + 1) * LANES] = upper[:, j * LANES : (j + 1) * LANES]
-
-    loads[2].wait()
-    loads[3].wait()
-    pl.semaphore_wait(barrier, 30)
-
-    stage_a = []
-    for index, (mx, my) in enumerate(plane):
-        px, py = flip(x, mx, 2), flip(y, my, 2)
-        copy = remote(
-            l4.at[px], r4.at[y, x], a_send.at[index], a_recv.at[index], place(px, py, w)
-        )
-        copy.start()
-        stage_a.append(copy)
-
     def lanes(index):
         return pl.ds(pl.multiple_of(index * LANES, LANES), LANES)
+
+    loads = []
+    for index, (src, dst) in enumerate((
+        (k_hbm, k_ref),
+        (v_hbm, v_ref),
+        (k_hbm.at[:, lanes(x)], kvb.at[x, :, pl.ds(0, LANES)]),
+        (v_hbm.at[:, lanes(x)], kvb.at[x, :, pl.ds(LANES, LANES)]),
+        (q_hbm.at[:, lanes(x)], qb.at[x]),
+        (g_hbm.at[:, lanes(x)], gb.at[x]),
+    )):
+        copy = pltpu.make_async_copy(src, dst, loc.at[index])
+        copy.start()
+        loads.append(copy)
+    pl.semaphore_wait(barrier, 30)
 
     def token_copies(mask):
         px = flip(x, mask, 2)
         device = place(px, y, w)
         pairs = (
-            (k_ref, kvb.at[x, :, pl.ds(0, LANES)]),
-            (v_ref, kvb.at[x, :, pl.ds(LANES, LANES)]),
-            (q_ref, qb.at[x]),
-            (g_ref, gb.at[x]),
+            (k_hbm, kvb.at[x, :, pl.ds(0, LANES)]),
+            (v_hbm, kvb.at[x, :, pl.ds(LANES, LANES)]),
+            (q_hbm, qb.at[x]),
+            (g_hbm, gb.at[x]),
         )
         return [
             remote(
@@ -258,24 +242,28 @@
         ]
 
     moves = {mask: token_copies(mask) for mask in (1, 2, 3)}
-    for i in range(3):
-        moves[1][i].start()
-        moves[3][i].start()
-    stage_c = []
-    for mx in range(4):
-        px = flip(x, mx, 2)
-        copy = remote(l3.at[px], kv3sib.at[x], c_send.at[mx], c_recv.at[mx], place(px, sib, w))
-        copy.start()
-        stage_c.append(copy)
-    for i in range(3):
-        moves[2][i].start()
-    for mask in (1, 3, 2):
-        moves[mask][3].start()
-
-    kvb[x, :, :LANES] = k_ref[:, lanes(x)]
-    kvb[x, :, LANES:] = v_ref[:, lanes(x)]
-    qb[x] = q_ref[:, lanes(x)]
-    gb[x] = g_ref[:, lanes(x)]
+    moves[1][0].start()
+    moves[3][0].start()
+
+    for part, ref in ((0, k_ref), (1, v_ref)):
+        loads[part].wait()
+        rows = coarsen(coarsen(coarsen(coarsen(ref[...]))))
+        for j in range(4):
+            l4[j, :, part * LANES : (part + 1) * LANES] = rows[:, j * LANES : (j + 1) * LANES]
+    stage_a = []
+    for index, (mx, my) in enumerate(plane):
+        copy = remote(
+            l4.at[flip(x, mx, 2)], r4.at[y, x], a_send.at[index], a_recv.at[index],
+            place(flip(x, mx, 2), flip(y, my, 2), w),
+        )
+        copy.start()
+        stage_a.append(copy)
+
+    for mask, i in ((1, 1), (3, 1), (2, 0), (2, 1)):
+        moves[mask][i].start()
+    for i in (2, 3):
+        for mask in (1, 3, 2):
+            moves[mask][i].start()
     r4[y, x] = l4[x]
 
     def chunk_forward(slot):
@@ -284,9 +272,11 @@
         w0[slot] = weights
         w0p[slot], w0w[slot], w0t[slot] = peak, weighted, total
         qp[slot] = coarsen(q)
-        kvp[slot] = coarsen(kv)
-
+
+    for copy in loads[2:5]:
+        copy.wait()
     chunk_forward(x)
+    kvp[x] = coarsen(kvb[x])
 
     for copy in stage_a:
         copy.wait_recv()
@@ -302,7 +292,7 @@
 
     stage_b = []
     owns = (own5, own6, own7, own8)
-    for m in range(1, 16):
+    for m in range(15, 0, -1):
         up = m.bit_length() - 1
         count = 8 >> up
         start = 8 * up + (w % 2**up) * count
@@ -319,24 +309,30 @@
         w1p[unit], w1w[unit], w1t[unit] = peak, weighted, total
 
     for mask in (1, 3, 2):
-        for copy in moves[mask][:3]:
+        for copy in moves[mask][:2]:
             copy.wait_recv()
+        kvp[flip(x, mask, 2)] = coarsen(kvb[flip(x, mask, 2)])
+    kvp[4] = coarsen(kvp[0:2].reshape(256, 256))
+    kvp[5] = coarsen(kvp[2:4].reshape(256, 256))
+    own3[...] = coarsen(kvp[4:6].reshape(256, 256))
+    level3 = remote(own3, kv3sib, c_send.at[0], c_recv.at[0], place(x, sib, w))
+    level3.start()
+    for mask in (1, 3, 2):
+        moves[mask][2].wait_recv()
         chunk_forward(flip(x, mask, 2))
         if mask == 1:
             unit_forward(x, flip(x, 1, 2))
             unit_forward(flip(x, 1, 2), x)
+    qp[4] = coarsen(qp[0:2].reshape(256, LANES))
+    qp[5] = coarsen(qp[2:4].reshape(256, LANES))
+    qp[6] = coarsen(qp[4:6].reshape(256, LANES))
     unit_forward(flip(x, 3, 2), flip(x, 2, 2))
     unit_forward(flip(x, 2, 2), flip(x, 3, 2))
-    for copy in stage_c:
-        copy.wait_recv()
-    kvp[7] = kv3sib[...].reshape(LANES, 256)
-    qp[4] = coarsen(qp[0:2].reshape(256, LANES))
-    qp[5] = coarsen(qp[2:4].reshape(256, LANES))
-    kvp[4] = coarsen(kvp[0:2].reshape(256, 256))
-    kvp[5] = coarsen(kvp[2:4].reshape(256, 256))
-    qp[6] = coarsen(qp[4:6].reshape(256, LANES))
-    for unit in (4, 5, 6):
-        unit_forward(unit, unit ^ 1)
+    unit_forward(4, 5)
+    unit_forward(5, 4)
+    level3.wait_recv()
+    kvp[7] = kv3sib[...]
+    unit_forward(6, 7)
 
     qs = mm(half, qp[6])
     qs = jnp.concatenate([qs, jnp.zeros((64, LANES), F32)], axis=0)
@@ -429,8 +425,6 @@
             src, dst, o_send.at[kind, mask - 1], o_recv.at[kind, mask - 1], place(px, y, w)
         )
 
-    for mask in (1, 3, 2):
-        moves[mask][3].wait_recv()
     for mask in (1, 3, 2, 0):
         px = flip(x, mask, 2)
         crest, numer, denom, own, rest = merge(
@@ -438,21 +432,35 @@
         )
         inverse = 1.0 / denom
         ratio = numer * inverse
+        ob[px] = ratio.astype(BF16)
+        ratios[mask], inverses[mask] = ratio, inverse
+        w0p[px], w0t[px] = own, rest
+    outs = {(kind, mask): output_copy(kind, mask) for kind in range(3) for mask in (1, 3, 2)}
+    locals_ = [
+        pltpu.make_async_copy(ob.at[x], out_ref.at[:, lanes(x)], loc.at[0]),
+        pltpu.make_async_copy(oq.at[x], gq_ref.at[:, lanes(x)], loc.at[1]),
+        pltpu.make_async_copy(bk.at[x], bkr.at[x], loc.at[2]),
+        pltpu.make_async_copy(cs.at[x], cb.at[x], loc.at[3]),
+    ]
+    for mask in (1, 3, 2):
+        outs[0, mask].start()
+    locals_[0].start()
+
+    for mask in (1, 3, 2):
+        moves[mask][3].wait_recv()
+    loads[5].wait()
+    for mask in (1, 3, 2, 0):
+        px = flip(x, mask, 2)
         up = gb[px].astype(F32)
-        high, low = split2(up * ratio)
+        inverse = inverses[mask]
+        high, low = split2(up * ratios[mask])
         drift = -mm(jnp.concatenate([high, low], axis=1), head_sum) * inverse
         scaled = up * inverse
-        if mask:
-            ob[px] = ratio.astype(BF16)
-        else:
-            out_ref[:, lanes(x)] = ratio.astype(BF16)
+        own, rest = w0p[px], w0t[px]
         gw0[px] = (own * scaled).astype(BF16)
         gt0[px] = own * drift
         g1s[px] = paired(rest * scaled)
         d1s[px] = paired(rest * drift)
-    outs = {(kind, mask): output_copy(kind, mask) for kind in range(3) for mask in (1, 3, 2)}
-    for mask in (1, 3, 2):
-        outs[0, mask].start()
 
     g1, dd1 = g1s[...].reshape(512, LANES), d1s[...].reshape(512, LANES)
     gw1[0:4] = (own1 * g1).astype(BF16).reshape(4, LANES, LANES)
@@ -481,11 +489,11 @@
     gk_far = mm_tn(gs_blocks, q_stack)
     gv_far = mm_tn(blocks_s, grads_s[:, :LANES])
     far_grads = jnp.concatenate([gk_far, gv_far], axis=1)
-    g4s[...] = far_grads[:LANES].reshape(2, 64, 256)
+    s4[...] = far_grads[:LANES].astype(BF16).reshape(2, 64, 256)
     sb[...] = far_grads[LANES:].astype(BF16).reshape(32, 16, 256)
 
     back_b = []
-    for m in range(1, 16):
+    for m in range(15, 0, -1):
         up = m.bit_length() - 1
         count = 8 >> up
         pw = flip(w, m, 4)
@@ -510,6 +518,18 @@
         gq1[unit], gkv1[unit ^ 1] = attend_back(
             qp[unit], kvp[unit ^ 1], w1[unit], gw1[unit], gt1[unit]
         )
+
+    s3[...] = gkv1[7].astype(BF16)
+    back_y = [remote(s3, e3, ey_send.at[0], ey_recv.at[0], place(x, sib, w))]
+    for m in (2, 3):
+        py = flip(y, m, 2)
+        back_y.append(
+            remote(
+                s4.at[py % 2], e4.at[y_bit], ey_send.at[m - 1], ey_recv.at[m - 1], place(x, py, w)
+            )
+        )
+    for copy in back_y:
+        copy.start()
 
     run_q2 = gq1[4:6].reshape(256, LANES) + 0.5 * doubled(gq1[6] + run_q3)
     run_q1 = gq1[0:4].reshape(512, LANES) + 0.5 * doubled(run_q2)
@@ -527,16 +547,14 @@
         gq = (gq + 0.5 * doubled(m1[px])).astype(BF16)
         gk = (gkv[:, :LANES] + 0.5 * doubled(n1[px])).astype(BF16)
         gv = (gkv[:, LANES:] + 0.5 * doubled(d1[px])).astype(BF16)
+        oq[px] = gq
+        bk[px, :, :LANES] = gk
+        bk[px, :, LANES:] = gv
         if mask:
-            oq[px] = gq
-            bk[px, :, :LANES] = gk
-            bk[px, :, LANES:] = gv
             outs[1, mask].start()
             outs[2, mask].start()
-        else:
-            gq_ref[:, lanes(x)] = gq
-            bkr[x, :, :LANES] = gk
-            bkr[x, :, LANES:] = gv
+    locals_[1].start()
+    locals_[2].start()
 
     for copy in back_b:
         copy.wait_recv()
@@ -547,58 +565,78 @@
         inside = jnp.bitwise_and(col, (LANES >> up) - 1)
         gather.append(jnp.where(shr(row, up) == inside, 0.5**up, 0.0))
     gather = jnp.concatenate(gather, axis=1).astype(BF16)
-    run5 = mm(gather, rb[...].reshape(512, 256)).astype(BF16)
-    t4[...] = mm(spread_matrix(LANES, 0.5), run5).reshape(4, 64, 256)
-    m4s[y] = t4[y].astype(BF16).reshape(4, 16, 256)
-    other_pair = 2 * (1 - y_pair)
-    for half_index in range(2):
-        slot = other_pair + half_index
-        m4s[slot] = (t4[slot] + g4s[half_index]).astype(BF16).reshape(4, 16, 256)
-    near = mm(spread_matrix(64, 0.5), t4[sib].astype(BF16)) + gkv1[7]
-    m3s[...] = near.astype(BF16).reshape(4, 2, 16, 256)
-
-    back_a = []
-    for index, (mx, my) in enumerate(plane):
-        px, py = flip(x, mx, 2), flip(y, my, 2)
-        if my == 0:
-            src, dst = m4s.at[py, pl.ds(px, 1)], cb.at[x, pl.ds(0, 1)]
-        elif my == 1:
-            src, dst = m3s.at[px], cb.at[x, pl.ds(1, 2)]
-        else:
-            src, dst = m4s.at[py, pl.ds(px, 1)], cb.at[x, pl.ds(3 + y_bit, 1)]
-        copy = remote(src, dst, aa_send.at[index], aa_recv.at[index], place(px, py, w))
-        copy.start()
-        back_a.append(copy)
-    cb[x, 0] = m4s[y, x]
-
-    for copy in back_a:
+    s5[...] = mm(gather, rb[...].reshape(512, 256)).astype(BF16).reshape(4, 2, 16, 256)
+    for m in (1, 2, 3):
+        py = flip(y, m, 2)
+        copy = remote(s5.at[py], e5.at[y], e5_send.at[m - 1], e5_recv.at[m - 1], place(x, py, w))
+        copy.start()
+        back_y.append(copy)
+    e5[y] = s5[y]
+    fill = [jnp.where(row == col, 1.0, 0.0)]
+    inside = jnp.bitwise_and(col, 63)
+    fill.append(jnp.where(shr(row, 1) == inside, 0.5, 0.0))
+    inside = jnp.bitwise_and(col, 31)
+    fill.append(jnp.where(shr(row, 2) == inside, 0.25, 0.0))
+    fill = jnp.concatenate(fill, axis=1).astype(BF16)
+    for copy in back_y:
+        copy.wait_recv()
+    rows = jnp.concatenate([e3[...], e4[...].reshape(LANES, 256), e5[...].reshape(LANES, 256)], axis=0)
+    cs[...] = mm(fill, rows).astype(BF16).reshape(4, 2, 16, 256)
+    back_x = []
+    for m in (1, 3, 2):
+        px = flip(x, m, 2)
+        copy = remote(cs.at[px], cb.at[x], cx_send.at[m - 1], cx_recv.at[m - 1], place(px, y, w))
+        copy.start()
+        back_x.append(copy)
+    locals_[3].start()
+
+    for copy in back_x:
         copy.wait_recv()
     for copy in outs.values():
         copy.wait_recv()
-    for copies in (stage_a, stage_b, stage_c, back_b, back_a, outs.values(), *moves.values()):
+    for copy in locals_:
+        copy.wait()
+    for copies in (
+        stage_a, [level3], stage_b, back_b, back_y, back_x, outs.values(),
+        *moves.values(),
+    ):
         for copy in copies:
             copy.wait_send()
 
 
-def finish(out_v, gq_v, cb, bkr, out_ref, gq_ref, gk_ref, gv_ref, gk_v, gv_v, sems):
-    first = pltpu.make_async_copy(out_v, out_ref, sems.at[0])
-    second = pltpu.make_async_copy(gq_v, gq_ref, sems.at[1])
-    first.start()
-    second.start()
-    shape = (256, 80)
-    token, unit = iota(shape, 0), iota(shape, 1)
-    fine = (unit >= 16) & (unit < 48) & (shr(token, 3) == unit - 16)
-    coarse = ((unit < 16) | (unit >= 48)) & (shr(token, 4) == jnp.bitwise_and(unit, 15))
-    last = (jnp.where(fine, 0.125, 0.0) + jnp.where(coarse, 0.0625, 0.0)).astype(BF16)
+def finish(
+    out_h, gq_h, cb_h, bkr_h, out_ref, gq_ref, gk_ref, gv_ref,
+    out_v, gq_v, cb, bkr, gk_v, gv_v, sems, out_sems,
+):
+    moves = [
+        pltpu.make_async_copy(src, dst, sems.at[i])
+        for i, (src, dst) in enumerate(
+            ((cb_h, cb), (bkr_h, bkr), (out_h, out_v), (gq_h, gq_v))
+        )
+    ]
+    for copy in moves:
+        copy.start()
+    shape = (256, 32)
+    last = jnp.where(shr(iota(shape, 0), 3) == iota(shape, 1), 0.125, 0.0).astype(BF16)
+    moves[2].wait()
+    moves[3].wait()
+    writes = [
+        pltpu.make_async_copy(out_v, out_ref, out_sems.at[0]),
+        pltpu.make_async_copy(gq_v, gq_ref, out_sems.at[1]),
+    ]
+    for copy in writes:
+        copy.start()
+    moves[0].wait()
+    moves[1].wait()
     for j in range(4):
-        total = mm(last, cb[j].reshape(80, 256)) + bkr[j].astype(F32)
+        total = mm(last, cb[j].reshape(32, 256)) + bkr[j].astype(F32)
         gk_v[:, j * LANES : (j + 1) * LANES] = total[:, :LANES].astype(BF16)
         gv_v[:, j * LANES : (j + 1) * LANES] = total[:, LANES:].astype(BF16)
-    third = pltpu.make_async_copy(gk_v, gk_ref, sems.at[2])
-    fourth = pltpu.make_async_copy(gv_v, gv_ref, sems.at[3])
-    third.start()
-    fourth.start()
-    for copy in (first, second, third, fourth):
+    for i, (src, dst) in enumerate(((gk_v, gk_ref), (gv_v, gv_ref))):
+        copy = pltpu.make_async_copy(src, dst, out_sems.at[2 + i])
+        copy.start()
+        writes.append(copy)
+    for copy in writes:
         copy.wait()
 
 
@@ -614,9 +652,9 @@
 
     dma = pltpu.SemaphoreType.DMA
     scratch = [
-        b16(256, 512), b16(256, 512), b16(256, 512), b16(256, 512),
+        b16(256, 512), b16(256, 512),
         b16(4, 256, 128), b16(4, 256, 256), b16(4, 256, 128),
-        b16(4, 32, 256), b16(4, 16, 256), b16(4, 32, 256), b16(4, 4, 16, 256),
+        b16(4, 16, 256), b16(128, 256), b16(128, 256), b16(4, 4, 16, 256),
         b16(8, 16, 256), b16(4, 16, 256), b16(2, 16, 256), b16(1, 16, 256),
         b16(32, 16, 256),
         b16(7, 128, 128), b16(8, 128, 256),
@@ -629,33 +667,38 @@
         b16(4, 256, 128), b16(4, 256, 128), b16(4, 256, 256),
         f32(7, 128, 128), f32(8, 128, 256),
         b16(32, 16, 256), b16(32, 16, 256),
-        f32(4, 64, 256), b16(4, 2, 16, 256), b16(4, 4, 16, 256), f32(2, 64, 256),
-        dma((4, 3)), dma((4, 3)), dma((15,)), dma((15,)), dma((4,)), dma((4,)),
-        dma((15,)), dma((15,)), dma((15,)), dma((15,)), dma((15,)), dma((15,)),
-        dma((3, 3)), dma((3, 3)), dma((4,)),
+        b16(128, 256), b16(2, 64, 256), b16(4, 2, 16, 256),
+        b16(128, 256), b16(2, 64, 256), b16(4, 2, 16, 256),
+        b16(4, 2, 16, 256), f32(4, 256, 128), f32(4, 256, 128),
+        dma((4, 3)), dma((4, 3)), dma((15,)), dma((15,)),
+        dma((1,)), dma((1,)), dma((15,)), dma((15,)), dma((15,)), dma((15,)),
+        dma((3,)), dma((3,)), dma((3,)), dma((3,)), dma((3,)), dma((3,)),
+        dma((3, 3)), dma((3, 3)), dma((6,)),
     ]
-    vmem = pl.BlockSpec(memory_space=pltpu.VMEM)
     hbm = pl.BlockSpec(memory_space=pltpu.HBM)
     parts = pl.pallas_call(
         kernel,
         out_shape=(
             whole, whole,
-            jax.ShapeDtypeStruct((4, 5, 16, 256), BF16), jax.ShapeDtypeStruct((4, 256, 256), BF16),
+            jax.ShapeDtypeStruct((4, 2, 16, 256), BF16), jax.ShapeDtypeStruct((4, 256, 256), BF16),
         ),
         in_specs=[hbm] * 4,
-        out_specs=(vmem,) * 4,
+        out_specs=(hbm,) * 4,
         scratch_shapes=scratch,
         compiler_params=pltpu.CompilerParams(
-            collective_id=0, has_side_effects=True, vmem_limit_bytes=40 * 2**20
+            collective_id=0, has_side_effects=True, vmem_limit_bytes=56 * 2**20
         ),
     )(query, key_in, value_in, grad_out)
     return pl.pallas_call(
         finish,
         out_shape=(whole,) * 4,
-        in_specs=[vmem] * 4,
+        in_specs=[hbm] * 4,
         out_specs=(hbm,) * 4,
-        scratch_shapes=[b16(256, 512), b16(256, 512), dma((4,))],
-        compiler_params=pltpu.CompilerParams(vmem_limit_bytes=8 * 2**20),
+        scratch_shapes=[
+            b16(256, 512), b16(256, 512), b16(4, 2, 16, 256), b16(4, 256, 256),
+            b16(256, 512), b16(256, 512), dma((4,)), dma((4,)),
+        ],
+        compiler_params=pltpu.CompilerParams(vmem_limit_bytes=56 * 2**20),
     )(*parts)
 
 

time: 52.2 us -> 46.8 us (0.90)
  local copies, waits for them, and re-layouts: 3.79 us -> 0 us
  Pallas kernels: 47.2 us -> 46.1 us
    unnamed x8 -> x0, local copies, waits for them, and re-layouts: 3.79 us -> none
    pallas_call x1, Pallas kernels: 46.1 us -> 43.7 us  [shards(): pl.pallas_call(kernel, out_shape=(whole, whole, jax.ShapeDtypeStruct((4,...]
    pallas_call x1, Pallas kernels: 1.11 us -> 2.35 us  [shards(): pl.pallas_call(finish, out_shape=(whole,) * 4, in_specs=[hbm] * 4, out_sp...]
where the time goes in v2:
time: 46.8 us; the launch traced here: 46.7 us
  Pallas kernels  46.1 us (99%)
  between operations  0.64 us (1%)
    pallas_call x1, Pallas kernels, shards(): pl.pallas_call(kernel, out_shape=(whole, whole, jax.ShapeDtypeStruct((4,...  43.7 us
    pallas_call x1, Pallas kernels, shards(): pl.pallas_call(finish, out_shape=(whole,) * 4, in_specs=[hbm] * 4, out_sp...  2.35 us

profile of v2, /device:TPU:6, one launch (start us, length us, event | category | flops | bytes accessed | tf_op | source)
XLA Modules:
  0.0 46.7 jit_solution(15706728185797441722)
XLA Ops:
  0.6 43.7 %shard_map.75 = (bf16[256,512]{1,0:T(8,128)(2,1)}, bf16[256,512]{1,0:T(8,128)(2,1)}, bf16[4,2,16,256]{3,2,1,0:T(8,128)(2,1)}, bf16[4,256,256]{2,1,0:T(8,128)(2,1)}) custom-call(bf16[256,512]{1,0:T(8,128)(2,1)} %q_hbm.1, bf16[256,512]{1,0:T(8,128)(2,1)} %k_hbm.1, bf16[256,512]{1,0:T(8,128)(2,1)} %v_hbm.1, bf16[256,512]{1,0:T(8,128)(2,1)} %g_hbm.1), custom_call_target="tpu_custom_call" | custom-call | tf_op jit(solution)/shard_map/pallas_call | solution.py:679
  44.4 2.4 %shard_map.76 = (bf16[256,512]{1,0:T(8,128)(2,1)}, bf16[256,512]{1,0:T(8,128)(2,1)}, bf16[256,512]{1,0:T(8,128)(2,1)}, bf16[256,512]{1,0:T(8,128)(2,1)}) custom-call(bf16[256,512]{1,0:T(8,128)(2,1)} %get-tuple-element.8.out_h, bf16[256,512]{1,0:T(8,128)(2,1)} %get-tuple-element.9.gq_h, bf16[4,2,16,256]{3,2,1,0:T(8,128)(2,1)} %get-tuple-element.10.cb_h, ...), custom_call_target="tpu_custom_call" | custom-call | tf_op jit(solution)/shard_map/pallas_call | solution.py:692

commit v3 on v2

--- a/solution.py
+++ b/solution.py
@@ -174,11 +174,11 @@
 
 
 def kernel(
-    q_hbm, k_hbm, v_hbm, g_hbm, out_ref, gq_ref, cb, bkr,
+    q_hbm, k_hbm, v_hbm, g_hbm, out_ref, gq_ref, cb, bkr, bvr,
     k_ref, v_ref, qb, kvb, gb, l4, own3, kv3sib, r4, own5, own6, own7, own8, rf,
     qp, kvp, w0, w1, w0w, w0p, w0t, w1w, w1p, w1t,
     m1, n1, d1, gw0, gt0, gw1, gt1, sp, g1s, d1s,
-    ob, oq, bk, gq1, gkv1, sb, rb, s3, s4, s5, e3, e4, e5, cs, ratios, inverses,
+    ob, oq, bk, bv, gq1, gkv1, sb, rb, s3, s4, s5, e3, e4, e5, cs, ratios, inverses,
     p_send, p_recv, a_send, a_recv, c_send, c_recv, b_send, b_recv, bb_send, bb_recv,
     ey_send, ey_recv, e5_send, e5_recv, cx_send, cx_recv, o_send, o_recv, loc,
 ):
@@ -419,8 +419,10 @@
             src, dst = ob.at[px], out_ref.at[:, lanes(x)]
         elif kind == 1:
             src, dst = oq.at[px], gq_ref.at[:, lanes(x)]
+        elif kind == 2:
+            src, dst = bk.at[px], bkr.at[x]
         else:
-            src, dst = bk.at[px], bkr.at[x]
+            src, dst = bv.at[px], bvr.at[x]
         return remote(
             src, dst, o_send.at[kind, mask - 1], o_recv.at[kind, mask - 1], place(px, y, w)
         )
@@ -435,12 +437,13 @@
         ob[px] = ratio.astype(BF16)
         ratios[mask], inverses[mask] = ratio, inverse
         w0p[px], w0t[px] = own, rest
-    outs = {(kind, mask): output_copy(kind, mask) for kind in range(3) for mask in (1, 3, 2)}
+    outs = {(kind, mask): output_copy(kind, mask) for kind in range(4) for mask in (1, 3, 2)}
     locals_ = [
         pltpu.make_async_copy(ob.at[x], out_ref.at[:, lanes(x)], loc.at[0]),
         pltpu.make_async_copy(oq.at[x], gq_ref.at[:, lanes(x)], loc.at[1]),
         pltpu.make_async_copy(bk.at[x], bkr.at[x], loc.at[2]),
         pltpu.make_async_copy(cs.at[x], cb.at[x], loc.at[3]),
+        pltpu.make_async_copy(bv.at[x], bvr.at[x], loc.at[4]),
     ]
     for mask in (1, 3, 2):
         outs[0, mask].start()
@@ -548,13 +551,15 @@
         gk = (gkv[:, :LANES] + 0.5 * doubled(n1[px])).astype(BF16)
         gv = (gkv[:, LANES:] + 0.5 * doubled(d1[px])).astype(BF16)
         oq[px] = gq
-        bk[px, :, :LANES] = gk
-        bk[px, :, LANES:] = gv
+        bk[px] = gk
+        bv[px] = gv
         if mask:
             outs[1, mask].start()
             outs[2, mask].start()
+            outs[3, mask].start()
     locals_[1].start()
     locals_[2].start()
+    locals_[4].start()
 
     for copy in back_b:
         copy.wait_recv()
@@ -604,36 +609,21 @@
             copy.wait_send()
 
 
-def finish(
-    out_h, gq_h, cb_h, bkr_h, out_ref, gq_ref, gk_ref, gv_ref,
-    out_v, gq_v, cb, bkr, gk_v, gv_v, sems, out_sems,
-):
-    moves = [
-        pltpu.make_async_copy(src, dst, sems.at[i])
-        for i, (src, dst) in enumerate(
-            ((cb_h, cb), (bkr_h, bkr), (out_h, out_v), (gq_h, gq_v))
-        )
+def finish(out_v, gq_v, cb, bk, bv, out_ref, gq_ref, gk_ref, gv_ref, gk_v, gv_v, sems):
+    writes = [
+        pltpu.make_async_copy(out_v, out_ref, sems.at[0]),
+        pltpu.make_async_copy(gq_v, gq_ref, sems.at[1]),
     ]
-    for copy in moves:
+    for copy in writes:
         copy.start()
     shape = (256, 32)
     last = jnp.where(shr(iota(shape, 0), 3) == iota(shape, 1), 0.125, 0.0).astype(BF16)
-    moves[2].wait()
-    moves[3].wait()
-    writes = [
-        pltpu.make_async_copy(out_v, out_ref, out_sems.at[0]),
-        pltpu.make_async_copy(gq_v, gq_ref, out_sems.at[1]),
-    ]
-    for copy in writes:
-        copy.start()
-    moves[0].wait()
-    moves[1].wait()
     for j in range(4):
-        total = mm(last, cb[j].reshape(32, 256)) + bkr[j].astype(F32)
-        gk_v[:, j * LANES : (j + 1) * LANES] = total[:, :LANES].astype(BF16)
-        gv_v[:, j * LANES : (j + 1) * LANES] = total[:, LANES:].astype(BF16)
+        total = mm(last, cb[j].reshape(32, 256))
+        gk_v[:, j * LANES : (j + 1) * LANES] = (total[:, :LANES] + bk[j].astype(F32)).astype(BF16)
+        gv_v[:, j * LANES : (j + 1) * LANES] = (total[:, LANES:] + bv[j].astype(F32)).astype(BF16)
     for i, (src, dst) in enumerate(((gk_v, gk_ref), (gv_v, gv_ref))):
-        copy = pltpu.make_async_copy(src, dst, out_sems.at[2 + i])
+        copy = pltpu.make_async_copy(src, dst, sems.at[2 + i])
         copy.start()
         writes.append(copy)
     for copy in writes:
@@ -664,7 +654,7 @@
         f32(4, 128, 128), f32(4, 128, 128), f32(4, 128, 128),
         b16(4, 256, 128), f32(4, 256, 128), b16(7, 128, 128), f32(7, 128, 128),
         f32(48, 512, 128), f32(4, 128, 128), f32(4, 128, 128),
-        b16(4, 256, 128), b16(4, 256, 128), b16(4, 256, 256),
+        b16(4, 256, 128), b16(4, 256, 128), b16(4, 256, 128), b16(4, 256, 128),
         f32(7, 128, 128), f32(8, 128, 256),
         b16(32, 16, 256), b16(32, 16, 256),
         b16(128, 256), b16(2, 64, 256), b16(4, 2, 16, 256),
@@ -673,32 +663,31 @@
         dma((4, 3)), dma((4, 3)), dma((15,)), dma((15,)),
         dma((1,)), dma((1,)), dma((15,)), dma((15,)), dma((15,)), dma((15,)),
         dma((3,)), dma((3,)), dma((3,)), dma((3,)), dma((3,)), dma((3,)),
-        dma((3, 3)), dma((3, 3)), dma((6,)),
+        dma((4, 3)), dma((4, 3)), dma((6,)),
     ]
     hbm = pl.BlockSpec(memory_space=pltpu.HBM)
+    vmem = pl.BlockSpec(memory_space=pltpu.VMEM)
+    anywhere = pl.BlockSpec(memory_space=pl.ANY)
     parts = pl.pallas_call(
         kernel,
         out_shape=(
             whole, whole,
-            jax.ShapeDtypeStruct((4, 2, 16, 256), BF16), jax.ShapeDtypeStruct((4, 256, 256), BF16),
+            jax.ShapeDtypeStruct((4, 2, 16, 256), BF16), *[jax.ShapeDtypeStruct((4, 256, 128), BF16)] * 2,
         ),
         in_specs=[hbm] * 4,
-        out_specs=(hbm,) * 4,
+        out_specs=(anywhere,) * 5,
         scratch_shapes=scratch,
         compiler_params=pltpu.CompilerParams(
-            collective_id=0, has_side_effects=True, vmem_limit_bytes=56 * 2**20
+            collective_id=0, has_side_effects=True, vmem_limit_bytes=54036 * 2**10
         ),
     )(query, key_in, value_in, grad_out)
     return pl.pallas_call(
         finish,
         out_shape=(whole,) * 4,
-        in_specs=[hbm] * 4,
+        in_specs=[vmem] * 5,
         out_specs=(hbm,) * 4,
-        scratch_shapes=[
-            b16(256, 512), b16(256, 512), b16(4, 2, 16, 256), b16(4, 256, 256),
-            b16(256, 512), b16(256, 512), dma((4,)), dma((4,)),
-        ],
-        compiler_params=pltpu.CompilerParams(vmem_limit_bytes=56 * 2**20),
+        scratch_shapes=[b16(256, 512), b16(256, 512), dma((4,))],
+        compiler_params=pltpu.CompilerParams(vmem_limit_bytes=8 * 2**20),
     )(*parts)
 
 

time: 46.8 us -> 45.5 us (0.972)
  Pallas kernels: 46.1 us -> 44.8 us
    pallas_call x1, Pallas kernels: 2.35 us -> 1.1 us  [shards(): pl.pallas_call(finish, out_shape=(whole,) * 4, in_specs=[vmem] * 5, out_s...]
where the time goes in v3:
time: 45.5 us; the launch traced here: 45.4 us
  Pallas kernels  44.8 us (98%)
  between operations  0.64 us (1%)
    pallas_call x1, Pallas kernels, shards(): pl.pallas_call(kernel, out_shape=(whole, whole, jax.ShapeDtypeStruct((4,...  43.7 us
    pallas_call x1, Pallas kernels, shards(): pl.pallas_call(finish, out_shape=(whole,) * 4, in_specs=[vmem] * 5, out_s...  1.1 us

profile of v3, /device:TPU:6, one launch (start us, length us, event | category | flops | bytes accessed | tf_op | source)
XLA Modules:
  0.0 45.4 jit_solution(10914025539328146754)
XLA Ops:
  0.6 43.7 %shard_map.75 = (bf16[256,512]{1,0:T(8,128)(2,1)S(1)}, bf16[256,512]{1,0:T(8,128)(2,1)S(1)}, bf16[4,2,16,256]{3,2,1,0:T(8,128)(2,1)S(1)}, bf16[4,256,128]{2,1,0:T(8,128)(2,1)S(1)}, bf16[4,256,128]{2,1,0:T(8,128)(2,1)S(1)}) custom-call(bf16[256,512]{1,0:T(8,128)(2,1)} %q_hbm.1, bf16[256,512]{1,0:T(8,128)(2,1)} %k_hbm.1, bf16[256,512]{1,0:T(8,128)(2,1)} %v_hbm.1, ...), custom_call_target="tpu_custom_call" | custom-call | tf_op jit(solution)/shard_map/pallas_call | solution.py:671
  44.4 1.1 %shard_map.76 = (bf16[256,512]{1,0:T(8,128)(2,1)}, bf16[256,512]{1,0:T(8,128)(2,1)}, bf16[256,512]{1,0:T(8,128)(2,1)}, bf16[256,512]{1,0:T(8,128)(2,1)}) custom-call(bf16[256,512]{1,0:T(8,128)(2,1)S(1)} %get-tuple-element.9.out_v, bf16[256,512]{1,0:T(8,128)(2,1)S(1)} %get-tuple-element.10.gq_v, bf16[4,2,16,256]{3,2,1,0:T(8,128)(2,1)S(1)} %get-tuple-element.11.cb, ...), custom_call_target="tpu_custom_call" | custom-call | tf_op jit(solution)/shard_map/pallas_call | solution.py:684

commit v4 on v3

--- a/solution.py
+++ b/solution.py
@@ -449,11 +449,11 @@
         outs[0, mask].start()
     locals_[0].start()
 
-    for mask in (1, 3, 2):
-        moves[mask][3].wait_recv()
     loads[5].wait()
-    for mask in (1, 3, 2, 0):
+    for mask in (0, 1, 3, 2):
         px = flip(x, mask, 2)
+        if mask:
+            moves[mask][3].wait_recv()
         up = gb[px].astype(F32)
         inverse = inverses[mask]
         high, low = split2(up * ratios[mask])

time: 45.5 us -> 46 us (1.011)
  no operation moved by 1% of the time
where the time goes in v4:
time: 46 us; the launch traced here: 45.9 us
  Pallas kernels  45.2 us (98%)
  between operations  0.64 us (1%)
    pallas_call x1, Pallas kernels, shards(): pl.pallas_call(kernel, out_shape=(whole, whole, jax.ShapeDtypeStruct((4,...  44.1 us
    pallas_call x1, Pallas kernels, shards(): pl.pallas_call(finish, out_shape=(whole,) * 4, in_specs=[vmem] * 5, out_s...  1.09 us

profile of v4, /device:TPU:6, one launch (start us, length us, event | category | flops | bytes accessed | tf_op | source)
XLA Modules:
  0.0 45.9 jit_solution(6394967214529127402)
XLA Ops:
  0.6 44.1 %shard_map.75 = (bf16[256,512]{1,0:T(8,128)(2,1)S(1)}, bf16[256,512]{1,0:T(8,128)(2,1)S(1)}, bf16[4,2,16,256]{3,2,1,0:T(8,128)(2,1)S(1)}, bf16[4,256,128]{2,1,0:T(8,128)(2,1)S(1)}, bf16[4,256,128]{2,1,0:T(8,128)(2,1)S(1)}) custom-call(bf16[256,512]{1,0:T(8,128)(2,1)} %q_hbm.1, bf16[256,512]{1,0:T(8,128)(2,1)} %k_hbm.1, bf16[256,512]{1,0:T(8,128)(2,1)} %v_hbm.1, ...), custom_call_target="tpu_custom_call" | custom-call | tf_op jit(solution)/shard_map/pallas_call | solution.py:671
  44.8 1.1 %shard_map.76 = (bf16[256,512]{1,0:T(8,128)(2,1)}, bf16[256,512]{1,0:T(8,128)(2,1)}, bf16[256,512]{1,0:T(8,128)(2,1)}, bf16[256,512]{1,0:T(8,128)(2,1)}) custom-call(bf16[256,512]{1,0:T(8,128)(2,1)S(1)} %get-tuple-element.9.out_v, bf16[256,512]{1,0:T(8,128)(2,1)S(1)} %get-tuple-element.10.gq_v, bf16[4,2,16,256]{3,2,1,0:T(8,128)(2,1)S(1)} %get-tuple-element.11.cb, ...), custom_call_target="tpu_custom_call" | custom-call | tf_op jit(solution)/shard_map/pallas_call | solution.py:684
